TPU v7x, 32 devices: a whole 2x2x4 slice. The times are simulated.
32 devices in a mesh: grp: 4 (over z), shard: 2 (over x), tp: 4 (over y, core).
Axes of the slice: x: 2, y: 2, z: 4, core: 2. Of those that a mesh axis runs over, the one named last changes fastest.
Arguments:
- inner_weights: float32 [4, 2, 4096, 7168], P('grp', None, 'shard', 'tp'), may hold values from -6 to 6
- start_weights: float32 [2, 4096, 7168], P(None, 'shard', 'tp'), may hold values from -6 to 6
- momentum: float32 [2, 2, 4, 32, 64, 1792], P(None, None, None, ('grp', 'shard', 'tp')), may hold values from -6 to 6
Outputs:
- new_weights: float32 [2, 4096, 7168], P(None, 'shard', 'tp')
- new_momentum: float32 [2, 2, 4, 32, 64, 1792], P(None, None, None, ('grp', 'shard', 'tp'))
All inputs are finite; a program needn't handle non-finite values.
Results may differ from a plain program's by a relative error of at most 0.00002.
Values sent between devices are 32-bit elements; how exact they have to be, the bound alone decides.
No kernel may reach another device: no remote copies, remote signals or barrier semaphores. Data moves between devices by JAX's collectives and lax.ppermute only.
A program may use at most 192 MiB of HBM per device.

v0:
```python
import jax
import jax.numpy as jnp
from jax import lax
from jax.experimental import pallas as pl
from jax.sharding import PartitionSpec as P

OUTER_RATE = 0.7
MOMENTUM_COEF = 0.5
STEPS = 8


def blank(shape):
    return pl.pallas_call(
        lambda out: None,
        out_shape=jax.ShapeDtypeStruct(shape, jnp.float32),
        out_specs=pl.BlockSpec(memory_space=pl.ANY),
    )()


def body(inner_weights, start_weights, momentum):
    groups = lax.axis_size("grp")
    shards = lax.axis_size("shard")
    tp_size = lax.axis_size("tp")
    plane = shards * tp_size
    group = lax.axis_index("grp")
    place = lax.axis_index(("shard", "tp"))
    row_count, col_count = start_weights.shape[1:]
    q_rows = row_count // (groups * plane)
    steps = min(STEPS, plane)
    merge = plane // steps
    block = (q_rows, col_count)

    inner = inner_weights.reshape((2, groups, plane) + block)
    start = start_weights.reshape((2, groups, plane) + block)
    held = momentum.reshape((2, plane) + block)
    rightward = [(i, i + 1) for i in range(groups - 1)]
    leftward = [(i + 1, i) for i in range(groups - 1)]

    def lane(shift):
        return lax.rem(place + shift, plane)

    def shifts_of(step):
        return [step * merge + m for m in range(merge)]

    def join(parts):
        return parts[0] if len(parts) == 1 else jnp.concatenate(parts, axis=0)

    def rows_of(array, matrix, owner, step):
        def cut(shift):
            return lax.dynamic_slice(array, (matrix, owner, lane(shift), 0, 0), (1, 1, 1) + block).reshape(block)

        return join([cut(shift) for shift in shifts_of(step)])

    def own(matrix, owner, step):
        return rows_of(start, matrix, owner, step) - rows_of(inner, matrix, owner, step)

    def rotate(part, shift):
        if shift % plane == 0:
            return part
        return lax.ppermute(part, ("shard", "tp"), [(i, (i + shift) % plane) for i in range(plane)])

    new_weights = blank(start.shape)
    new_held = blank(held.shape)

    def write_weights(array, matrix, owner, step, value):
        for m, shift in enumerate(shifts_of(step)):
            part = value[m * q_rows : (m + 1) * q_rows]
            array = lax.dynamic_update_slice(array, part[None, None, None], (matrix, owner, lane(shift), 0, 0))
        return array

    def after(first, *arrays):
        return lax.optimization_barrier((*first, *arrays))[len(first) :]

    order = [(turn + 1) % steps for turn in range(steps)]
    zero = jnp.zeros((merge * q_rows, col_count), jnp.float32)
    from_left, from_right = [zero, zero], [zero, zero]
    arrived_left, arrived_right = [[], []], [[], []]
    moved, outgoing, transit = {}, {}, []
    payload = (zero,)

    def fetch(step):
        (here,) = after(payload, place)
        parts = []
        for shift in shifts_of(step):
            at = lax.rem(here + plane - shift, plane)
            halves = [lax.dynamic_slice(held, (matrix, at, 0, 0), (1, 1) + block)[0] for matrix in range(2)]
            parts.append(jnp.stack([half[0] for half in halves]))
        return ("fetch", step, [rotate(part, -shift) for part, shift in zip(parts, shifts_of(step))])

    def deliver(step):
        halves = after(payload, *outgoing[step])
        parts = []
        for m, shift in enumerate(shifts_of(step)):
            parts.append(jnp.stack([half[m * q_rows : (m + 1) * q_rows] for half in halves]))
        return ("deliver", step, [rotate(part, shift) for part, shift in zip(parts, shifts_of(step))])

    def land(array, step, parts):
        for shift, part in zip(shifts_of(step), parts):
            array = lax.dynamic_update_slice(array, part[:, None], (0, lane(plane - shift), 0, 0))
        return array

    for turn in range(steps + 1):
        for phase in range(1, groups + 1):
            if turn == steps and phase > groups - 2:
                break
            for matrix in range(2):
                in_turn = (phase - 1) * 2 + matrix
                tick = turn * groups * 2 + in_turn
                landed = [entry for entry in transit if entry[0] <= tick]
                transit = [entry for entry in transit if entry[0] > tick]
                values = after(payload, from_left[matrix], from_right[matrix], *[p for e in landed for p in e[3]])
                here_left, here_right, values = values[0], values[1], list(values[2:])
                for _, kind, step, parts in landed:
                    parts, values = values[: len(parts)], values[len(parts) :]
                    if kind == "fetch":
                        moved[step] = parts
                    else:
                        new_held = land(new_held, step, parts)
                step = order[turn] if turn < steps else None
                alone = None
                if turn == 0 and phase == 1:
                    (owner,) = after(payload, jnp.where(group == 0, groups - 1, 0))
                    alone = own(matrix, owner, step)
                    to_right = to_left = alone
                elif turn == steps and phase == groups - 2:
                    alone = jnp.where(group >= groups // 2, here_left, here_right)
                    to_right = to_left = alone
                elif phase < groups:
                    to_right, to_left = here_left, here_right
                    if turn < steps:
                        right_owner = jnp.minimum(groups - phase + group, groups - 1)
                        left_owner = jnp.maximum(group - (groups - phase), 0)
                        to_right = jnp.where(group < phase, to_right + own(matrix, right_owner, step), to_right)
                        to_left = jnp.where(groups - 1 - group < phase, to_left + own(matrix, left_owner, step), to_left)
                else:
                    total = own(matrix, group, step) + here_left + here_right
                    mean_diff = total / groups
                    old_momentum = join([part[matrix] for part in moved[step]])
                    new_momentum = MOMENTUM_COEF * old_momentum + mean_diff
                    update = OUTER_RATE * (mean_diff + MOMENTUM_COEF * new_momentum)
                    outgoing.setdefault(step, []).append(new_momentum)
                    fresh = rows_of(start, matrix, group, step) - update
                    new_weights = write_weights(new_weights, matrix, group, step, fresh)
                    to_right = to_left = fresh
                payload = (to_right, to_left)
                if alone is None:
                    from_left[matrix] = lax.ppermute(to_right, "grp", rightward)
                    from_right[matrix] = lax.ppermute(to_left, "grp", leftward)
                else:
                    outer = [(0, 1), (groups - 1, groups - 2)]
                    ends = [(groups - 2, groups - 1), (1, 0)]
                    from_left[matrix] = from_right[matrix] = lax.ppermute(alone, "grp", outer if turn == 0 else ends)
                if tick == 0:
                    transit.append((tick + groups,) + fetch(order[0]))
                if in_turn == 2 * groups - 2 and turn + 1 < steps:
                    transit.append((tick + groups,) + fetch(order[turn + 1]))
                if in_turn == groups - 2 and 0 < turn < steps:
                    transit.append((tick + groups,) + deliver(order[turn - 1]))
                if phase == groups:
                    arrived_left[matrix], arrived_right[matrix] = [], []
                arrived_left[matrix].append(from_left[matrix])
                arrived_right[matrix].append(from_right[matrix])
                if len(arrived_left[matrix]) == groups - 1 and turn > 0:
                    for hop in range(groups - 1):
                        fresh = jnp.where(
                            group > hop,
                            arrived_left[matrix][hop],
                            arrived_right[matrix][groups - 2 - hop],
                        )
                        owner = lax.rem(group + groups - 1 - hop, groups)
                        new_weights = write_weights(new_weights, matrix, owner, order[turn - 1], fresh)
    new_held = land(new_held, *deliver(order[-1])[1:])
    return (new_weights.reshape(start_weights.shape), new_held.reshape(momentum.shape))


def solution(mesh):
    in_specs = (
        P("grp", None, "shard", "tp"),
        P(None, "shard", "tp"),
        P(None, None, None, ("grp", "shard", "tp"), None, None),
    )
    out_specs = (P(None, "shard", "tp"), P(None, None, None, ("grp", "shard", "tp"), None, None))
    return jax.shard_map(body, mesh=mesh, in_specs=in_specs, out_specs=out_specs, check_vma=False)
```

profile of v0, /device:TPU:0, one launch (start us, length us, event | category | flops | bytes accessed | tf_op | source)
XLA Modules:
  0.0 709.0 jit_solution(10196058520968157740)
XLA Ops:
  2.6 4.9 collective-permute-start
  13.1 5.7 collective-permute-done
  82.3 4.6 collective-permute-start.15
  89.8 4.6 collective-permute-start.20
  103.1 4.6 collective-permute-start.19
  112.9 4.6 collective-permute-start.23
  163.2 4.6 collective-permute-start.33
  170.7 4.6 collective-permute-start.38
  176.8 4.7 collective-permute-done.34
  184.4 4.6 collective-permute-start.37
  194.2 4.6 collective-permute-start.41
  248.9 4.6 collective-permute-start.51
  270.9 4.6 collective-permute-start.55
  280.7 4.6 collective-permute-start.59
  310.0 4.6 collective-permute-start.65
  330.3 4.6 collective-permute-start.69
  353.1 4.6 collective-permute-start.73
  362.9 4.6 collective-permute-start.77
  415.1 4.6 collective-permute-start.87
  422.5 4.6 collective-permute-start.92
  436.0 5.0 collective-permute-start.91
  445.9 5.0 collective-permute-start.95
  461.7 4.6 collective-permute-start.99
  511.7 4.7 collective-permute-done.106
  519.3 4.6 collective-permute-start.109
  529.2 4.6 collective-permute-start.113
  560.5 4.6 collective-permute-start.119
  580.7 4.6 collective-permute-start.123
  603.5 4.6 collective-permute-start.126
  613.3 4.6 collective-permute-start.130
  682.9 7.5 %collective-permute-done.144 = f32[64,1792]{1,0:T(8,128)S(1)} collective-permute-done((f32[64,1792]{1,0:T(8,128)S(1)}, f32[64,1792]{1,0:T(8,128)S(1)}, u32[]{:S(2)}, u32[]{:S(2)}) %collective-permute-start.144) | collective-permute-done | bytes 458784 | tf_op jit(solution)/shard_map/ppermute | solution.py:148
  692.7 7.5 %collective-permute-done.142 = f32[64,1792]{1,0:T(8,128)S(1)} collective-permute-done((f32[64,1792]{1,0:T(8,128)S(1)}, f32[64,1792]{1,0:T(8,128)S(1)}, u32[]{:S(2)}, u32[]{:S(2)}) %collective-permute-start.142) | collective-permute-done | bytes 458784 | tf_op jit(solution)/shard_map/ppermute | solution.py:152
  (435 shorter events, 551.6 us)
Async XLA Ops:
  8.8 19.7 %collective-permute-start.1 = (f32[64,1792]{1,0:T(8,128)S(1)}, f32[64,1792]{1,0:T(8,128)S(1)}, u32[]{:S(2)}, u32[]{:S(2)}) collective-permute-start(f32[64,1792]{1,0:T(8,128)S(1)} %subtract_bitcast_fusion), channel_id=1, source_target_pairs={{0,8},{24,16},{1,9},{25,17},{2,10},{26,18},{3,11},{27,19},{4,12},{... | collective-permute-start | bytes 1376264 | tf_op jit(solution)/shard_map/ppermute | solution.py:152
  11.4 26.9 %collective-permute-start.4 = (f32[2,64,1792]{2,1,0:T(8,128)S(1)}, f32[2,64,1792]{2,1,0:T(8,128)S(1)}, u32[]{:S(2)}, u32[]{:S(2)}) collective-permute-start(f32[2,64,1792]{2,1,0:T(8,128)S(1)} %pad_maximum_fusion), channel_id=1, source_target_pairs={{0,7},{1,0},{2,1},{3,2},{4,3},{5,4},{6,5},{7,6},{8,15},{9,8},{10,9... | collective-permute-start | bytes 2752520 | tf_op jit(solution)/shard_map/ppermute | solution.py:60
  61.2 19.5 %collective-permute-start.11 = (f32[64,1792]{1,0:T(8,128)S(1)}, f32[64,1792]{1,0:T(8,128)S(1)}, u32[]{:S(2)}, u32[]{:S(2)}) collective-permute-start(f32[64,1792]{1,0:T(8,128)S(1)} %get-tuple-element.411), channel_id=1, source_target_pairs={{0,8},{8,16},{16,24},{1,9},{9,17},{17,25},{2,10},{10,18},{18,26},{... | collective-permute-start | bytes 1376264 | tf_op jit(solution)/shard_map/ppermute | solution.py:147
  78.2 22.0 %collective-permute-start.17 = (f32[2,64,1792]{2,1,0:T(8,128)S(1)}, f32[2,64,1792]{2,1,0:T(8,128)S(1)}, u32[]{:S(2)}, u32[]{:S(2)}) collective-permute-start(f32[2,64,1792]{2,1,0:T(8,128)S(1)} %pad_maximum_fusion.1), channel_id=1, source_target_pairs={{0,6},{1,7},{2,0},{3,1},{4,2},{5,3},{6,4},{7,5},{8,14},{9,15},{10,... | collective-permute-start | bytes 2752520 | tf_op jit(solution)/shard_map/ppermute | solution.py:60
  117.6 23.2 %collective-permute-start.26 = (f32[2,64,1792]{2,1,0:T(8,128)S(1)}, f32[2,64,1792]{2,1,0:T(8,128)S(1)}, u32[]{:S(2)}, u32[]{:S(2)}) collective-permute-start(f32[2,64,1792]{2,1,0:T(8,128)S(1)} %pad_maximum_fusion.2), channel_id=1, source_target_pairs={{0,1},{1,2},{2,3},{3,4},{4,5},{5,6},{6,7},{7,0},{8,9},{9,10},{10,1... | collective-permute-start | bytes 2752520 | tf_op jit(solution)/shard_map/ppermute | solution.py:60
  129.0 19.8 %collective-permute-start.27 = (f32[64,1792]{1,0:T(8,128)S(1)}, f32[64,1792]{1,0:T(8,128)S(1)}, u32[]{:S(2)}, u32[]{:S(2)}) collective-permute-start(f32[64,1792]{1,0:T(8,128)S(1)} %get-tuple-element.485), channel_id=1, source_target_pairs={{0,8},{8,16},{16,24},{1,9},{9,17},{17,25},{2,10},{10,18},{18,26},{... | collective-permute-start | bytes 1376264 | tf_op jit(solution)/shard_map/ppermute | solution.py:147
  159.4 22.1 %collective-permute-start.35 = (f32[2,64,1792]{2,1,0:T(8,128)S(1)}, f32[2,64,1792]{2,1,0:T(8,128)S(1)}, u32[]{:S(2)}, u32[]{:S(2)}) collective-permute-start(f32[2,64,1792]{2,1,0:T(8,128)S(1)} %pad_maximum_fusion.3), channel_id=1, source_target_pairs={{0,5},{1,6},{2,7},{3,0},{4,1},{5,2},{6,3},{7,4},{8,13},{9,14},{10,... | collective-permute-start | bytes 2752520 | tf_op jit(solution)/shard_map/ppermute | solution.py:60
  198.9 25.3 %collective-permute-start.44 = (f32[2,64,1792]{2,1,0:T(8,128)S(1)}, f32[2,64,1792]{2,1,0:T(8,128)S(1)}, u32[]{:S(2)}, u32[]{:S(2)}) collective-permute-start(f32[2,64,1792]{2,1,0:T(8,128)S(1)} %pad_maximum_fusion.4), channel_id=1, source_target_pairs={{0,2},{1,3},{2,4},{3,5},{4,6},{5,7},{6,0},{7,1},{8,10},{9,11},{10,... | collective-permute-start | bytes 2752520 | tf_op jit(solution)/shard_map/ppermute | solution.py:60
  203.1 21.1 %collective-permute-start.42 = (f32[64,1792]{1,0:T(8,128)S(1)}, f32[64,1792]{1,0:T(8,128)S(1)}, u32[]{:S(2)}, u32[]{:S(2)}) collective-permute-start(f32[64,1792]{1,0:T(8,128)S(1)} %get-tuple-element.475), channel_id=1, source_target_pairs={{0,8},{8,16},{16,24},{1,9},{9,17},{17,25},{2,10},{10,18},{18,26},{... | collective-permute-start | bytes 1376264 | tf_op jit(solution)/shard_map/ppermute | solution.py:147
  212.6 19.6 %collective-permute-start.45 = (f32[64,1792]{1,0:T(8,128)S(1)}, f32[64,1792]{1,0:T(8,128)S(1)}, u32[]{:S(2)}, u32[]{:S(2)}) collective-permute-start(f32[64,1792]{1,0:T(8,128)S(1)} %get-tuple-element.473), channel_id=1, source_target_pairs={{0,8},{8,16},{16,24},{1,9},{9,17},{17,25},{2,10},{10,18},{18,26},{... | collective-permute-start | bytes 1376264 | tf_op jit(solution)/shard_map/ppermute | solution.py:147
  227.7 19.5 %collective-permute-start.47 = (f32[64,1792]{1,0:T(8,128)S(1)}, f32[64,1792]{1,0:T(8,128)S(1)}, u32[]{:S(2)}, u32[]{:S(2)}) collective-permute-start(f32[64,1792]{1,0:T(8,128)S(1)} %get-tuple-element.395), channel_id=1, source_target_pairs={{0,8},{8,16},{16,24},{1,9},{9,17},{17,25},{2,10},{10,18},{18,26},{... | collective-permute-start | bytes 1376264 | tf_op jit(solution)/shard_map/ppermute | solution.py:147
  235.6 19.2 %collective-permute-start.49 = (f32[64,1792]{1,0:T(8,128)}, f32[64,1792]{1,0:T(8,128)S(1)}, u32[]{:S(2)}, u32[]{:S(2)}) collective-permute-start(f32[64,1792]{1,0:T(8,128)} %get-tuple-element.393), channel_id=1, source_target_pairs={{0,8},{8,16},{16,24},{1,9},{9,17},{17,25},{2,10},{10,18},{18,26},{... | collective-permute-start | bytes 1376264 | tf_op jit(solution)/shard_map/ppermute | solution.py:147
  242.9 22.5 %collective-permute-start.53 = (f32[2,64,1792]{2,1,0:T(8,128)S(1)}, f32[2,64,1792]{2,1,0:T(8,128)S(1)}, u32[]{:S(2)}, u32[]{:S(2)}) collective-permute-start(f32[2,64,1792]{2,1,0:T(8,128)S(1)} %pad_maximum_fusion.5), channel_id=1, source_target_pairs={{0,4},{1,5},{2,6},{3,7},{4,0},{5,1},{6,2},{7,3},{8,12},{9,13},{10,... | collective-permute-start | bytes 2752520 | tf_op jit(solution)/shard_map/ppermute | solution.py:60
  285.4 20.7 %collective-permute-start.62 = (f32[2,64,1792]{2,1,0:T(8,128)S(1)}, f32[2,64,1792]{2,1,0:T(8,128)S(1)}, u32[]{:S(2)}, u32[]{:S(2)}) collective-permute-start(f32[2,64,1792]{2,1,0:T(8,128)S(1)} %pad_maximum_fusion.6), channel_id=1, source_target_pairs={{0,3},{1,4},{2,5},{3,6},{4,7},{5,0},{6,1},{7,2},{8,11},{9,12},{10,... | collective-permute-start | bytes 2752520 | tf_op jit(solution)/shard_map/ppermute | solution.py:60
  296.9 19.0 %collective-permute-start.63 = (f32[64,1792]{1,0:T(8,128)S(1)}, f32[64,1792]{1,0:T(8,128)S(1)}, u32[]{:S(2)}, u32[]{:S(2)}) collective-permute-start(f32[64,1792]{1,0:T(8,128)S(1)} %get-tuple-element.461), channel_id=1, source_target_pairs={{0,8},{8,16},{16,24},{1,9},{9,17},{17,25},{2,10},{10,18},{18,26},{... | collective-permute-start | bytes 1376264 | tf_op jit(solution)/shard_map/ppermute | solution.py:147
  310.0 18.7 %collective-permute-start.65 = (f32[64,1792]{1,0:T(8,128)S(1)}, f32[64,1792]{1,0:T(8,128)S(1)}, u32[]{:S(2)}, u32[]{:S(2)}) collective-permute-start(f32[64,1792]{1,0:T(8,128)S(1)} %get-tuple-element.387), channel_id=1, source_target_pairs={{0,8},{8,16},{16,24},{1,9},{9,17},{17,25},{2,10},{10,18},{18,26},{... | collective-permute-start | bytes 1376264 | tf_op jit(solution)/shard_map/ppermute | solution.py:147
  338.9 18.8 %collective-permute-start.74 = (f32[64,1792]{1,0:T(8,128)S(1)}, f32[64,1792]{1,0:T(8,128)S(1)}, u32[]{:S(2)}, u32[]{:S(2)}) collective-permute-start(f32[64,1792]{1,0:T(8,128)S(1)} %get-tuple-element.457), channel_id=1, source_target_pairs={{0,8},{8,16},{16,24},{1,9},{9,17},{17,25},{2,10},{10,18},{18,26},{... | collective-permute-start | bytes 1376264 | tf_op jit(solution)/shard_map/ppermute | solution.py:147
  367.6 23.6 %collective-permute-start.80 = (f32[2,64,1792]{2,1,0:T(8,128)S(1)}, f32[2,64,1792]{2,1,0:T(8,128)S(1)}, u32[]{:S(2)}, u32[]{:S(2)}) collective-permute-start(f32[2,64,1792]{2,1,0:T(8,128)S(1)} %pad_maximum_fusion.8), channel_id=1, source_target_pairs={{0,4},{1,5},{2,6},{3,7},{4,0},{5,1},{6,2},{7,3},{8,12},{9,13},{10,... | collective-permute-start | bytes 2752520 | tf_op jit(solution)/shard_map/ppermute | solution.py:60
  371.5 19.7 %collective-permute-start.78 = (f32[64,1792]{1,0:T(8,128)S(1)}, f32[64,1792]{1,0:T(8,128)S(1)}, u32[]{:S(2)}, u32[]{:S(2)}) collective-permute-start(f32[64,1792]{1,0:T(8,128)S(1)} %get-tuple-element.451), channel_id=1, source_target_pairs={{0,8},{8,16},{16,24},{1,9},{9,17},{17,25},{2,10},{10,18},{18,26},{... | collective-permute-start | bytes 1376264 | tf_op jit(solution)/shard_map/ppermute | solution.py:147
  381.3 19.4 %collective-permute-start.81 = (f32[64,1792]{1,0:T(8,128)S(1)}, f32[64,1792]{1,0:T(8,128)S(1)}, u32[]{:S(2)}, u32[]{:S(2)}) collective-permute-start(f32[64,1792]{1,0:T(8,128)S(1)} %get-tuple-element.449), channel_id=1, source_target_pairs={{0,8},{8,16},{16,24},{1,9},{9,17},{17,25},{2,10},{10,18},{18,26},{... | collective-permute-start | bytes 1376264 | tf_op jit(solution)/shard_map/ppermute | solution.py:147
  394.8 18.7 %collective-permute-start.83 = (f32[64,1792]{1,0:T(8,128)S(1)}, f32[64,1792]{1,0:T(8,128)S(1)}, u32[]{:S(2)}, u32[]{:S(2)}) collective-permute-start(f32[64,1792]{1,0:T(8,128)S(1)} %get-tuple-element.379), channel_id=1, source_target_pairs={{0,8},{8,16},{16,24},{1,9},{9,17},{17,25},{2,10},{10,18},{18,26},{... | collective-permute-start | bytes 1376264 | tf_op jit(solution)/shard_map/ppermute | solution.py:147
  411.2 19.3 %collective-permute-start.89 = (f32[2,64,1792]{2,1,0:T(8,128)S(1)}, f32[2,64,1792]{2,1,0:T(8,128)S(1)}, u32[]{:S(2)}, u32[]{:S(2)}) collective-permute-start(f32[2,64,1792]{2,1,0:T(8,128)S(1)} %pad_maximum_fusion.9), channel_id=1, source_target_pairs={{0,2},{1,3},{2,4},{3,5},{4,6},{5,7},{6,0},{7,1},{8,10},{9,11},{10,... | collective-permute-start | bytes 2752520 | tf_op jit(solution)/shard_map/ppermute | solution.py:60
  450.9 21.8 %collective-permute-start.98 = (f32[2,64,1792]{2,1,0:T(8,128)S(1)}, f32[2,64,1792]{2,1,0:T(8,128)S(1)}, u32[]{:S(2)}, u32[]{:S(2)}) collective-permute-start(f32[2,64,1792]{2,1,0:T(8,128)S(1)} %pad_maximum_fusion.10), channel_id=1, source_target_pairs={{0,5},{1,6},{2,7},{3,0},{4,1},{5,2},{6,3},{7,4},{8,13},{9,14},{10,... | collective-permute-start | bytes 2752520 | tf_op jit(solution)/shard_map/ppermute | solution.py:60
  461.7 20.5 %collective-permute-start.99 = (f32[64,1792]{1,0:T(8,128)S(1)}, f32[64,1792]{1,0:T(8,128)S(1)}, u32[]{:S(2)}, u32[]{:S(2)}) collective-permute-start(f32[64,1792]{1,0:T(8,128)S(1)} %get-tuple-element.437), channel_id=1, source_target_pairs={{0,8},{8,16},{16,24},{1,9},{9,17},{17,25},{2,10},{10,18},{18,26},{... | collective-permute-start | bytes 1376264 | tf_op jit(solution)/shard_map/ppermute | solution.py:147
  518.0 19.6 %collective-permute-start.108 = (f32[64,1792]{1,0:T(8,128)S(1)}, f32[64,1792]{1,0:T(8,128)S(1)}, u32[]{:S(2)}, u32[]{:S(2)}) collective-permute-start(f32[64,1792]{1,0:T(8,128)S(1)} %get-tuple-element.431), channel_id=1, source_target_pairs={{8,0},{16,8},{24,16},{9,1},{17,9},{25,17},{10,2},{18,10},{26,18},{... | collective-permute-start | bytes 1376264 | tf_op jit(solution)/shard_map/ppermute | solution.py:148
  533.8 23.1 %collective-permute-start.116 = (f32[2,64,1792]{2,1,0:T(8,128)S(1)}, f32[2,64,1792]{2,1,0:T(8,128)S(1)}, u32[]{:S(2)}, u32[]{:S(2)}) collective-permute-start(f32[2,64,1792]{2,1,0:T(8,128)S(1)} %pad_maximum_fusion.12), channel_id=1, source_target_pairs={{0,6},{1,7},{2,0},{3,1},{4,2},{5,3},{6,4},{7,5},{8,14},{9,15},{10,... | collective-permute-start | bytes 2752520 | tf_op jit(solution)/shard_map/ppermute | solution.py:60
  547.5 18.8 %collective-permute-start.117 = (f32[64,1792]{1,0:T(8,128)S(1)}, f32[64,1792]{1,0:T(8,128)S(1)}, u32[]{:S(2)}, u32[]{:S(2)}) collective-permute-start(f32[64,1792]{1,0:T(8,128)S(1)} %get-tuple-element.425), channel_id=1, source_target_pairs={{0,8},{8,16},{16,24},{1,9},{9,17},{17,25},{2,10},{10,18},{18,26},{... | collective-permute-start | bytes 1376264 | tf_op jit(solution)/shard_map/ppermute | solution.py:147
  560.5 18.6 %collective-permute-start.119 = (f32[64,1792]{1,0:T(8,128)S(1)}, f32[64,1792]{1,0:T(8,128)S(1)}, u32[]{:S(2)}, u32[]{:S(2)}) collective-permute-start(f32[64,1792]{1,0:T(8,128)S(1)} %get-tuple-element.363), channel_id=1, source_target_pairs={{0,8},{8,16},{16,24},{1,9},{9,17},{17,25},{2,10},{10,18},{18,26},{... | collective-permute-start | bytes 1376264 | tf_op jit(solution)/shard_map/ppermute | solution.py:147
  618.0 21.9 %collective-permute-start.133 = (f32[2,64,1792]{2,1,0:T(8,128)S(1)}, f32[2,64,1792]{2,1,0:T(8,128)S(1)}, u32[]{:S(2)}, u32[]{:S(2)}) collective-permute-start(f32[2,64,1792]{2,1,0:T(8,128)S(1)} %pad_maximum_fusion.14), channel_id=1, source_target_pairs={{0,7},{1,0},{2,1},{3,2},{4,3},{5,4},{6,5},{7,6},{8,15},{9,8},{10,9... | collective-permute-start | bytes 2752520 | tf_op jit(solution)/shard_map/ppermute | solution.py:60
  628.8 18.7 %collective-permute-start.134 = (f32[64,1792]{1,0:T(8,128)S(1)}, f32[64,1792]{1,0:T(8,128)S(1)}, u32[]{:S(2)}, u32[]{:S(2)}) collective-permute-start(f32[64,1792]{1,0:T(8,128)S(1)} %get-tuple-element.413), channel_id=1, source_target_pairs={{0,8},{8,16},{16,24},{1,9},{9,17},{17,25},{2,10},{10,18},{18,26},{... | collective-permute-start | bytes 1376264 | tf_op jit(solution)/shard_map/ppermute | solution.py:147
  661.3 19.3 %collective-permute-start.141 = (f32[64,1792]{1,0:T(8,128)S(1)}, f32[64,1792]{1,0:T(8,128)S(1)}, u32[]{:S(2)}, u32[]{:S(2)}) collective-permute-start(f32[64,1792]{1,0:T(8,128)S(1)} %collective-permute-done.137), channel_id=1, source_target_pairs={{8,0},{16,8},{24,16},{9,1},{17,9},{25,17},{10,2},{18,10},{26,18},{... | collective-permute-start | bytes 1376264 | tf_op jit(solution)/shard_map/ppermute | solution.py:148
  680.6 19.6 %collective-permute-start.142 = (f32[64,1792]{1,0:T(8,128)S(1)}, f32[64,1792]{1,0:T(8,128)S(1)}, u32[]{:S(2)}, u32[]{:S(2)}) collective-permute-start(f32[64,1792]{1,0:T(8,128)S(1)} %broadcast_select_fusion.1), channel_id=1, source_target_pairs={{16,24},{8,0},{17,25},{9,1},{18,26},{10,2},{19,27},{11,3},{20,28},... | collective-permute-start | bytes 1376264 | tf_op jit(solution)/shard_map/ppermute | solution.py:152
  (120 other events, 1898.9 us)
where the time goes:
time: 719 us; the launch traced here: 709 us
  starting transfers between devices  366 us (51%)
  other arithmetic  172 us (24%)
  waiting for transfers between devices  145 us (20%)
  local copies, waits for them, and re-layouts  23.8 us (3%)
    ppermute x64, starting transfers between devices, body(): from_left[matrix] = lax.ppermute(to_right, 'grp', rightward)  260 us
    ppermute x64, waiting for transfers between devices, body(): from_right[matrix] = lax.ppermute(to_left, 'grp', leftward)  96.3 us
    ppermute x64, starting transfers between devices, body(): from_right[matrix] = lax.ppermute(to_left, 'grp', leftward)  83.1 us
    dynamic_update_slice x64, other arithmetic, write_weights(): lax.dynamic_update_slice(array, part[None, None, None], (matrix, owner, l...  71.2 us
    select_n x32, other arithmetic, body(): jnp.where(groups - 1 - group < phase, to_left + own(matrix, left_owner, s...  50.9 us
    ppermute x64, waiting for transfers between devices, body(): from_left[matrix] = lax.ppermute(to_right, 'grp', rightward)  22.6 us
    select_n x14, other arithmetic, body(): jnp.where(group < phase, to_right + own(matrix, right_owner, step), to_ri...  22.5 us
    add x16, other arithmetic, body(): new_momentum = MOMENTUM_COEF * old_momentum + mean_diff  22.2 us
  transfers between devices with their start and end apart: 146, of which 59 were waited for; matrix products, arithmetic and copies ran while one was open for 27% of the time, Pallas kernels for 0%

commit v1 on v0

--- a/solution.py
+++ b/solution.py
@@ -2,6 +2,7 @@
 import jax.numpy as jnp
 from jax import lax
 from jax.experimental import pallas as pl
+from jax.experimental.pallas import tpu as pltpu
 from jax.sharding import PartitionSpec as P
 
 OUTER_RATE = 0.7
@@ -15,6 +16,55 @@
         out_shape=jax.ShapeDtypeStruct(shape, jnp.float32),
         out_specs=pl.BlockSpec(memory_space=pl.ANY),
     )()
+
+
+def put_rows(array, matrix, group, lanes, own, from_left, from_right):
+    groups = array.shape[1]
+    hops = groups - 1
+    q_rows = array.shape[3]
+
+    def kernel(scalars, own, *rest):
+        left, right, out, sems = rest[:hops], rest[hops : 2 * hops], rest[2 * hops + 1], rest[2 * hops + 2]
+        group = scalars[0]
+
+        def copies(source, owner, slot):
+            return [
+                pltpu.make_async_copy(
+                    source.at[pl.ds(m * q_rows, q_rows)], out.at[matrix, owner, scalars[1 + m]], sems.at[slot, m]
+                )
+                for m in range(len(lanes))
+            ]
+
+        for copy in copies(own, group, hops):
+            copy.start()
+        for hop in range(hops):
+            owner = lax.rem(group + hops - hop, groups)
+
+            @pl.when(group > hop)
+            def _():
+                for copy in copies(left[hop], owner, hop):
+                    copy.start()
+
+            @pl.when(group <= hop)
+            def _():
+                for copy in copies(right[hops - 1 - hop], owner, hop):
+                    copy.start()
+
+        for slot in range(groups):
+            for copy in copies(own, group, slot):
+                copy.wait()
+
+    anywhere = pl.BlockSpec(memory_space=pl.ANY)
+    size = own.size * 4
+    return pl.pallas_call(
+        kernel,
+        out_shape=jax.ShapeDtypeStruct(array.shape, array.dtype),
+        in_specs=[pl.BlockSpec(memory_space=pltpu.SMEM)] + [anywhere] * (2 * groups),
+        out_specs=anywhere,
+        scratch_shapes=[pltpu.SemaphoreType.DMA((groups, len(lanes)))],
+        input_output_aliases={2 * groups: 0},
+        cost_estimate=pl.CostEstimate(flops=0, bytes_accessed=2 * groups * size, transcendentals=0),
+    )(jnp.stack([group, *lanes]).astype(jnp.int32), own, *from_left, *from_right, array)
 
 
 def body(inner_weights, start_weights, momentum):
@@ -62,12 +112,6 @@
     new_weights = blank(start.shape)
     new_held = blank(held.shape)
 
-    def write_weights(array, matrix, owner, step, value):
-        for m, shift in enumerate(shifts_of(step)):
-            part = value[m * q_rows : (m + 1) * q_rows]
-            array = lax.dynamic_update_slice(array, part[None, None, None], (matrix, owner, lane(shift), 0, 0))
-        return array
-
     def after(first, *arrays):
         return lax.optimization_barrier((*first, *arrays))[len(first) :]
 
@@ -75,7 +119,7 @@
     zero = jnp.zeros((merge * q_rows, col_count), jnp.float32)
     from_left, from_right = [zero, zero], [zero, zero]
     arrived_left, arrived_right = [[], []], [[], []]
-    moved, outgoing, transit = {}, {}, []
+    kept, moved, outgoing, transit = [None, None], {}, {}, []
     payload = (zero,)
 
     def fetch(step):
@@ -139,9 +183,8 @@
                     new_momentum = MOMENTUM_COEF * old_momentum + mean_diff
                     update = OUTER_RATE * (mean_diff + MOMENTUM_COEF * new_momentum)
                     outgoing.setdefault(step, []).append(new_momentum)
-                    fresh = rows_of(start, matrix, group, step) - update
-                    new_weights = write_weights(new_weights, matrix, group, step, fresh)
-                    to_right = to_left = fresh
+                    kept[matrix] = rows_of(start, matrix, group, step) - update
+                    to_right = to_left = kept[matrix]
                 payload = (to_right, to_left)
                 if alone is None:
                     from_left[matrix] = lax.ppermute(to_right, "grp", rightward)
@@ -150,25 +193,19 @@
                     outer = [(0, 1), (groups - 1, groups - 2)]
                     ends = [(groups - 2, groups - 1), (1, 0)]
                     from_left[matrix] = from_right[matrix] = lax.ppermute(alone, "grp", outer if turn == 0 else ends)
-                if tick == 0:
-                    transit.append((tick + groups,) + fetch(order[0]))
-                if in_turn == 2 * groups - 2 and turn + 1 < steps:
-                    transit.append((tick + groups,) + fetch(order[turn + 1]))
-                if in_turn == groups - 2 and 0 < turn < steps:
-                    transit.append((tick + groups,) + deliver(order[turn - 1]))
+                if in_turn == 0 and turn < steps:
+                    transit.append((tick + 3,) + fetch(order[turn]))
+                if in_turn == 3 and 0 < turn < steps:
+                    transit.append((tick + 5,) + deliver(order[turn - 1]))
                 if phase == groups:
                     arrived_left[matrix], arrived_right[matrix] = [], []
                 arrived_left[matrix].append(from_left[matrix])
                 arrived_right[matrix].append(from_right[matrix])
                 if len(arrived_left[matrix]) == groups - 1 and turn > 0:
-                    for hop in range(groups - 1):
-                        fresh = jnp.where(
-                            group > hop,
-                            arrived_left[matrix][hop],
-                            arrived_right[matrix][groups - 2 - hop],
-                        )
-                        owner = lax.rem(group + groups - 1 - hop, groups)
-                        new_weights = write_weights(new_weights, matrix, owner, order[turn - 1], fresh)
+                    lanes = [lane(shift) for shift in shifts_of(order[turn - 1])]
+                    new_weights = put_rows(
+                        new_weights, matrix, group, lanes, kept[matrix], arrived_left[matrix], arrived_right[matrix]
+                    )
     new_held = land(new_held, *deliver(order[-1])[1:])
     return (new_weights.reshape(start_weights.shape), new_held.reshape(momentum.shape))
 

time: 719 us -> 1610 us (2.24)
  Pallas kernels: 0.01 us -> 918 us
  waiting for transfers between devices: 145 us -> 49.5 us
  starting transfers between devices: 366 us -> 432 us
    pallas_call x0 -> x16, Pallas kernels: none -> 918 us  [put_rows(): pl.pallas_call(kernel, out_shape=jax.ShapeDtypeStruct(array.shape, array....]
    ppermute x64, waiting for transfers between devices: 96.3 us -> 14.7 us  [body(): from_right[matrix] = lax.ppermute(to_left, 'grp', leftward)]
    dynamic_update_slice x64 -> x0, other arithmetic: 71.2 us -> none  [write_weights(): lax.dynamic_update_slice(array, part[None, None, None], (matrix, owner, l...]
    ppermute x64, starting transfers between devices: 260 us -> 326 us  [body(): from_left[matrix] = lax.ppermute(to_right, 'grp', rightward)]
    select_n x32 -> x46, other arithmetic: 50.9 us -> 102 us  [body(): jnp.where(groups - 1 - group < phase, to_left + own(matrix, left_owner, s...]
    sub x0 -> x16, other arithmetic: none -> 28.2 us  [body(): kept[matrix] = rows_of(start, matrix, group, step) - update]
    select_n x14 -> x0, other arithmetic: 22.5 us -> none  [body(): jnp.where(group < phase, to_right + own(matrix, right_owner, step), to_ri...]
  transfers between devices with their start and end apart: 146 -> 146, of which waited for: 59 -> 34; matrix products, arithmetic and copies ran while one was open for 27% -> 12% of each run, Pallas kernels for 0% -> 54%
where the time goes in v1:
time: 1610 us; the launch traced here: 1600 us
  Pallas kernels  918 us (57%)
  starting transfers between devices  432 us (27%)
  other arithmetic  169 us (10%)
  waiting for transfers between devices  49.5 us (3%)
  local copies, waits for them, and re-layouts  27.6 us (2%)
    pallas_call x16, Pallas kernels, put_rows(): pl.pallas_call(kernel, out_shape=jax.ShapeDtypeStruct(array.shape, array....  918 us
    ppermute x64, starting transfers between devices, body(): from_left[matrix] = lax.ppermute(to_right, 'grp', rightward)  326 us
    select_n x46, other arithmetic, body(): jnp.where(groups - 1 - group < phase, to_left + own(matrix, left_owner, s...  102 us
    ppermute x64, starting transfers between devices, body(): from_right[matrix] = lax.ppermute(to_left, 'grp', leftward)  82.3 us
  transfers between devices with their start and end apart: 146, of which 34 were waited for; matrix products, arithmetic and copies ran while one was open for 12% of the time, Pallas kernels for 54%

profile of v1, /device:TPU:0, one launch (start us, length us, event | category | flops | bytes accessed | tf_op | source)
XLA Modules:
  0.0 1599.3 jit_solution(15981420097733204961)
XLA Ops:
  82.2 5.7 collective-permute-start.15
  113.1 5.8 collective-permute-start.22
  129.5 57.4 %shard_map.51.rest_6_ = f32[2,4,8,64,1792]{4,3,2,1,0:T(8,128)} custom-call(s32[2]{0:T(128)} %pad_add_fusion.7.scalars, f32[64,1792]{1,0:T(8,128)} %copy-done.54, f32[64,1792]{1,0:T(8,128)} %copy-done.25, f32[64,1792]{1,0:T(8,128)} %collective-permute-done.15.rest_1_, f32[64,1792]{1,0:T(8,128)} %copy-done.50, ...), custom_call_target="tpu_custom_call", output_to_operand_aliasing={{}: (8, {})} | custom-call | bytes 3670016 | tf_op jit(solution)/shard_map/pallas_call | solution.py:59
  190.1 5.4 collective-permute-start.26
  205.6 57.4 %shard_map.52.rest_6_ = f32[2,4,8,64,1792]{4,3,2,1,0:T(8,128)} custom-call(s32[2]{0:T(128)} %pad_add_fusion.7.scalars, f32[64,1792]{1,0:T(8,128)} %bitcast_subtract_fusion.3.own, f32[64,1792]{1,0:T(8,128)} %copy-done.16, f32[64,1792]{1,0:T(8,128)} %copy-done.38, f32[64,1792]{1,0:T(8,128)} %collective-permute-done.22.rest_2_, ...), custom_call_target="tpu_custom_call", output_to_operand_aliasing={{}: (8, {})} | custom-call | bytes 3670016 | tf_op jit(solution)/shard_map/pallas_call | solution.py:59
  307.9 5.8 collective-permute-start.40
  317.9 5.6 collective-permute-start.42
  327.4 57.4 %shard_map.53.rest_6_ = f32[2,4,8,64,1792]{4,3,2,1,0:T(8,128)} custom-call(s32[2]{0:T(128)} %pad_add_fusion.6.scalars, f32[64,1792]{1,0:T(8,128)} %bitcast_subtract_fusion.5.own, f32[64,1792]{1,0:T(8,128)} %collective-permute-done.28.rest_0_, f32[64,1792]{1,0:T(8,128)} %collective-permute-done.33.rest_1_, ...), custom_call_target="tpu_custom_call", output_to_operand_aliasing={{}: (8, {})} | custom-call | bytes 3670016 | tf_op jit(solution)/shard_map/pallas_call | solution.py:59
  388.0 5.4 collective-permute-start.44
  403.4 57.4 %shard_map.54.rest_6_ = f32[2,4,8,64,1792]{4,3,2,1,0:T(8,128)} custom-call(s32[2]{0:T(128)} %pad_add_fusion.6.scalars, f32[64,1792]{1,0:T(8,128)} %bitcast_subtract_fusion.7.own, f32[64,1792]{1,0:T(8,128)} %copy-done.13, f32[64,1792]{1,0:T(8,128)} %copy-done.39, f32[64,1792]{1,0:T(8,128)} %collective-permute-done.40.rest_2_, ...), custom_call_target="tpu_custom_call", output_to_operand_aliasing={{}: (8, {})} | custom-call | bytes 3670016 | tf_op jit(solution)/shard_map/pallas_call | solution.py:59
  506.2 5.8 collective-permute-start.58
  516.2 5.6 collective-permute-start.60
  522.9 57.4 %shard_map.55.rest_6_ = f32[2,4,8,64,1792]{4,3,2,1,0:T(8,128)} custom-call(s32[2]{0:T(128)} %get-tuple-element.491.scalars, f32[64,1792]{1,0:T(8,128)} %bitcast_subtract_fusion.9.own, f32[64,1792]{1,0:T(8,128)} %collective-permute-done.46.rest_0_, f32[64,1792]{1,0:T(8,128)} %collective-permute-done.51.rest_1_, ...), custom_call_target="tpu_custom_call", output_to_operand_aliasing={{}: (8, {})} | custom-call | bytes 3670016 | tf_op jit(solution)/shard_map/pallas_call | solution.py:59
  583.5 5.4 collective-permute-start.62
  598.9 57.4 %shard_map.56.rest_6_ = f32[2,4,8,64,1792]{4,3,2,1,0:T(8,128)} custom-call(s32[2]{0:T(128)} %get-tuple-element.491.scalars, f32[64,1792]{1,0:T(8,128)} %bitcast_subtract_fusion.11.own, f32[64,1792]{1,0:T(8,128)} %copy-done.14, f32[64,1792]{1,0:T(8,128)} %copy-done.40, f32[64,1792]{1,0:T(8,128)} %collective-permute-done.58.rest_2_, ...), custom_call_target="tpu_custom_call", output_to_operand_aliasing={{}: (8, {})} | custom-call | bytes 3670016 | tf_op jit(solution)/shard_map/pallas_call | solution.py:59
  701.3 5.8 collective-permute-start.76
  717.7 57.4 %shard_map.57.rest_6_ = f32[2,4,8,64,1792]{4,3,2,1,0:T(8,128)} custom-call(s32[2]{0:T(128)} %get-tuple-element.490.scalars, f32[64,1792]{1,0:T(8,128)} %bitcast_subtract_fusion.13.own, f32[64,1792]{1,0:T(8,128)} %collective-permute-done.64.rest_0_, f32[64,1792]{1,0:T(8,128)} %collective-permute-done.69.rest_1_, ...), custom_call_target="tpu_custom_call", output_to_operand_aliasing={{}: (8, {})} | custom-call | bytes 3670016 | tf_op jit(solution)/shard_map/pallas_call | solution.py:59
  778.3 5.4 collective-permute-start.80
  793.8 57.4 %shard_map.58.rest_6_ = f32[2,4,8,64,1792]{4,3,2,1,0:T(8,128)} custom-call(s32[2]{0:T(128)} %get-tuple-element.490.scalars, f32[64,1792]{1,0:T(8,128)} %bitcast_subtract_fusion.15.own, f32[64,1792]{1,0:T(8,128)} %copy-done.11, f32[64,1792]{1,0:T(8,128)} %copy-done.36, f32[64,1792]{1,0:T(8,128)} %collective-permute-done.76.rest_2_, ...), custom_call_target="tpu_custom_call", output_to_operand_aliasing={{}: (8, {})} | custom-call | bytes 3670016 | tf_op jit(solution)/shard_map/pallas_call | solution.py:59
  912.2 57.4 %shard_map.59.rest_6_ = f32[2,4,8,64,1792]{4,3,2,1,0:T(8,128)} custom-call(s32[2]{0:T(128)} %get-tuple-element.489.scalars, f32[64,1792]{1,0:T(8,128)} %bitcast_subtract_fusion.17.own, f32[64,1792]{1,0:T(8,128)} %collective-permute-done.82.rest_0_, f32[64,1792]{1,0:T(8,128)} %collective-permute-done.87.rest_1_, ...), custom_call_target="tpu_custom_call", output_to_operand_aliasing={{}: (8, {})} | custom-call | bytes 3670016 | tf_op jit(solution)/shard_map/pallas_call | solution.py:59
  988.2 57.4 %shard_map.60.rest_6_ = f32[2,4,8,64,1792]{4,3,2,1,0:T(8,128)} custom-call(s32[2]{0:T(128)} %get-tuple-element.489.scalars, f32[64,1792]{1,0:T(8,128)} %bitcast_subtract_fusion.19.own, f32[64,1792]{1,0:T(8,128)} %copy-done.12, f32[64,1792]{1,0:T(8,128)} %copy-done.41, f32[64,1792]{1,0:T(8,128)} %collective-permute-done.94.rest_2_, ...), custom_call_target="tpu_custom_call", output_to_operand_aliasing={{}: (8, {})} | custom-call | bytes 3670016 | tf_op jit(solution)/shard_map/pallas_call | solution.py:59
  1090.7 5.8 collective-permute-start.112
  1100.8 5.6 collective-permute-start.114
  1110.0 57.4 %shard_map.61.rest_6_ = f32[2,4,8,64,1792]{4,3,2,1,0:T(8,128)} custom-call(s32[2]{0:T(128)} %get-tuple-element.488.scalars, f32[64,1792]{1,0:T(8,128)} %bitcast_subtract_fusion.21.own, f32[64,1792]{1,0:T(8,128)} %collective-permute-done.100.rest_0_, f32[64,1792]{1,0:T(8,128)} %collective-permute-done.105.rest_1_, ...), custom_call_target="tpu_custom_call", output_to_operand_aliasing={{}: (8, {})} | custom-call | bytes 3670016 | tf_op jit(solution)/shard_map/pallas_call | solution.py:59
  1170.6 5.4 collective-permute-start.116
  1185.3 57.4 %shard_map.62.rest_6_ = f32[2,4,8,64,1792]{4,3,2,1,0:T(8,128)} custom-call(s32[2]{0:T(128)} %get-tuple-element.488.scalars, f32[64,1792]{1,0:T(8,128)} %bitcast_subtract_fusion.23.own, f32[64,1792]{1,0:T(8,128)} %copy-done.10, f32[64,1792]{1,0:T(8,128)} %copy-done.37, f32[64,1792]{1,0:T(8,128)} %collective-permute-done.112.rest_2_, ...), custom_call_target="tpu_custom_call", output_to_operand_aliasing={{}: (8, {})} | custom-call | bytes 3670016 | tf_op jit(solution)/shard_map/pallas_call | solution.py:59
  1323.7 5.8 collective-permute-start.135
  1338.5 57.4 %shard_map.63.rest_6_ = f32[2,4,8,64,1792]{4,3,2,1,0:T(8,128)} custom-call(s32[2]{0:T(128)} %pad_add_fusion.1.scalars, f32[64,1792]{1,0:T(8,128)} %bitcast_subtract_fusion.25.own, f32[64,1792]{1,0:T(8,128)} %copy-done.1, f32[64,1792]{1,0:T(8,128)} %collective-permute-done.123.rest_1_, f32[64,1792]{1,0:T(8,128)} %copy-done.27, ...), custom_call_target="tpu_custom_call", output_to_operand_aliasing={{}: (8, {})} | custom-call | bytes 3670016 | tf_op jit(solution)/shard_map/pallas_call | solution.py:59
  1395.9 57.4 %shard_map.64.rest_6_ = f32[2,4,8,64,1792]{4,3,2,1,0:T(8,128)} custom-call(s32[2]{0:T(128)} %pad_add_fusion.1.scalars, f32[64,1792]{1,0:T(8,128)} %bitcast_subtract_fusion.27.own, f32[64,1792]{1,0:T(8,128)} %copy-done.3, f32[64,1792]{1,0:T(8,128)} %copy-done.23, f32[64,1792]{1,0:T(8,128)} %copy-done.29, ...), custom_call_target="tpu_custom_call", output_to_operand_aliasing={{}: (8, {})} | custom-call | bytes 3670016 | tf_op jit(solution)/shard_map/pallas_call | solution.py:59
  1464.2 9.3 collective-permute-done.143.rest_4_
  1483.4 57.4 %shard_map.65.rest_6_ = f32[2,4,8,64,1792]{4,3,2,1,0:T(8,128)} custom-call(s32[2]{0:T(128)} %pad_add_fusion.scalars, f32[64,1792]{1,0:T(8,128)} %copy-done.55, f32[64,1792]{1,0:T(8,128)} %collective-permute-done.136.rest_0_, f32[64,1792]{1,0:T(8,128)} %collective-permute-done.141.rest_1_, f32[64,1792]{1,0:T(8,128)} %copy-done.59, ...), custom_call_target="tpu_custom_call", output_to_operand_aliasing={{}: (8, {})} | custom-call | bytes 3670016 | tf_op jit(solution)/shard_map/pallas_call | solution.py:59
  1541.7 57.4 %shard_map.66 = f32[2,4,8,64,1792]{4,3,2,1,0:T(8,128)} custom-call(s32[2]{0:T(128)} %pad_add_fusion.scalars, f32[64,1792]{1,0:T(8,128)} %copy-done.56, f32[64,1792]{1,0:T(8,128)} %collective-permute-done.135.rest_0_, f32[64,1792]{1,0:T(8,128)} %copy-done.57, f32[64,1792]{1,0:T(8,128)} %copy-done.60, ...), custom_call_target="tpu_custom_call", output_to_operand_aliasing={{}: (8, {})} | custom-call | bytes 3670016 | tf_op jit(solution)/shard_map/pallas_call | solution.py:59
  (519 shorter events, 584.5 us)
Async XLA Ops:
  111.8 75.2 %collective-permute-start.23 = (f32[64,1792]{1,0:T(8,128)}, f32[64,1792]{1,0:T(8,128)}, u32[]{:S(2)}, u32[]{:S(2)}) collective-permute-start(f32[64,1792]{1,0:T(8,128)} %get-tuple-element.456), channel_id=1, source_target_pairs={{8,0},{16,8},{24,16},{9,1},{17,9},{25,17},{10,2},{18,10},{26,18},{... | collective-permute-start | bytes 1376264 | tf_op jit(solution)/shard_map/ppermute | solution.py:191
  113.1 73.9 %collective-permute-start.22 = (f32[64,1792]{1,0:T(8,128)}, f32[64,1792]{1,0:T(8,128)}, u32[]{:S(2)}, u32[]{:S(2)}) collective-permute-start(f32[64,1792]{1,0:T(8,128)} %get-tuple-element.457), channel_id=1, source_target_pairs={{0,8},{8,16},{16,24},{1,9},{9,17},{17,25},{2,10},{10,18},{18,26},{... | collective-permute-start | bytes 1376264 | tf_op jit(solution)/shard_map/ppermute | solution.py:190
  121.8 73.7 %collective-permute-start.25 = (f32[64,1792]{1,0:T(8,128)}, f32[64,1792]{1,0:T(8,128)}, u32[]{:S(2)}, u32[]{:S(2)}) collective-permute-start(f32[64,1792]{1,0:T(8,128)} %get-tuple-element.454), channel_id=1, source_target_pairs={{8,0},{16,8},{24,16},{9,1},{17,9},{25,17},{10,2},{18,10},{26,18},{... | collective-permute-start | bytes 1376264 | tf_op jit(solution)/shard_map/ppermute | solution.py:191
  129.4 142.8 %collective-permute-start.30 = (f32[2,64,1792]{2,1,0:T(8,128)}, f32[2,64,1792]{2,1,0:T(8,128)}, u32[]{:S(2)}, u32[]{:S(2)}) collective-permute-start(f32[2,64,1792]{2,1,0:T(8,128)} %pad_maximum_fusion.2), channel_id=1, source_target_pairs={{0,1},{1,2},{2,3},{3,4},{4,5},{5,6},{6,7},{7,0},{8,9},{9,10},{10,1... | collective-permute-start | bytes 2752520 | tf_op jit(solution)/shard_map/ppermute | solution.py:110
  188.8 74.1 %collective-permute-start.27 = (f32[64,1792]{1,0:T(8,128)S(1)}, f32[64,1792]{1,0:T(8,128)S(1)}, u32[]{:S(2)}, u32[]{:S(2)}) collective-permute-start(f32[64,1792]{1,0:T(8,128)S(1)} %get-tuple-element.452), channel_id=1, source_target_pairs={{8,0},{16,8},{24,16},{9,1},{17,9},{25,17},{10,2},{18,10},{26,18},{... | collective-permute-start | bytes 1376264 | tf_op jit(solution)/shard_map/ppermute | solution.py:191
  306.6 78.2 %collective-permute-start.41 = (f32[64,1792]{1,0:T(8,128)}, f32[64,1792]{1,0:T(8,128)}, u32[]{:S(2)}, u32[]{:S(2)}) collective-permute-start(f32[64,1792]{1,0:T(8,128)} %get-tuple-element.444), channel_id=1, source_target_pairs={{8,0},{16,8},{24,16},{9,1},{17,9},{25,17},{10,2},{18,10},{26,18},{... | collective-permute-start | bytes 1376264 | tf_op jit(solution)/shard_map/ppermute | solution.py:191
  307.9 76.9 %collective-permute-start.40 = (f32[64,1792]{1,0:T(8,128)}, f32[64,1792]{1,0:T(8,128)}, u32[]{:S(2)}, u32[]{:S(2)}) collective-permute-start(f32[64,1792]{1,0:T(8,128)} %get-tuple-element.445), channel_id=1, source_target_pairs={{0,8},{8,16},{16,24},{1,9},{9,17},{17,25},{2,10},{10,18},{18,26},{... | collective-permute-start | bytes 1376264 | tf_op jit(solution)/shard_map/ppermute | solution.py:190
  316.6 76.7 %collective-permute-start.43 = (f32[64,1792]{1,0:T(8,128)}, f32[64,1792]{1,0:T(8,128)}, u32[]{:S(2)}, u32[]{:S(2)}) collective-permute-start(f32[64,1792]{1,0:T(8,128)} %get-tuple-element.442), channel_id=1, source_target_pairs={{8,0},{16,8},{24,16},{9,1},{17,9},{25,17},{10,2},{18,10},{26,18},{... | collective-permute-start | bytes 1376264 | tf_op jit(solution)/shard_map/ppermute | solution.py:191
  317.9 75.4 %collective-permute-start.42 = (f32[64,1792]{1,0:T(8,128)}, f32[64,1792]{1,0:T(8,128)}, u32[]{:S(2)}, u32[]{:S(2)}) collective-permute-start(f32[64,1792]{1,0:T(8,128)} %get-tuple-element.443), channel_id=1, source_target_pairs={{0,8},{8,16},{16,24},{1,9},{9,17},{17,25},{2,10},{10,18},{18,26},{... | collective-permute-start | bytes 1376264 | tf_op jit(solution)/shard_map/ppermute | solution.py:190
  324.6 145.5 %collective-permute-start.48 = (f32[2,64,1792]{2,1,0:T(8,128)}, f32[2,64,1792]{2,1,0:T(8,128)}, u32[]{:S(2)}, u32[]{:S(2)}) collective-permute-start(f32[2,64,1792]{2,1,0:T(8,128)} %pad_maximum_fusion.4), channel_id=1, source_target_pairs={{0,2},{1,3},{2,4},{3,5},{4,6},{5,7},{6,0},{7,1},{8,10},{9,11},{10,... | collective-permute-start | bytes 2752520 | tf_op jit(solution)/shard_map/ppermute | solution.py:110
  386.7 74.1 %collective-permute-start.45 = (f32[64,1792]{1,0:T(8,128)S(1)}, f32[64,1792]{1,0:T(8,128)S(1)}, u32[]{:S(2)}, u32[]{:S(2)}) collective-permute-start(f32[64,1792]{1,0:T(8,128)S(1)} %get-tuple-element.440), channel_id=1, source_target_pairs={{8,0},{16,8},{24,16},{9,1},{17,9},{25,17},{10,2},{18,10},{26,18},{... | collective-permute-start | bytes 1376264 | tf_op jit(solution)/shard_map/ppermute | solution.py:191
  504.9 75.4 %collective-permute-start.59 = (f32[64,1792]{1,0:T(8,128)}, f32[64,1792]{1,0:T(8,128)}, u32[]{:S(2)}, u32[]{:S(2)}) collective-permute-start(f32[64,1792]{1,0:T(8,128)} %get-tuple-element.432), channel_id=1, source_target_pairs={{8,0},{16,8},{24,16},{9,1},{17,9},{25,17},{10,2},{18,10},{26,18},{... | collective-permute-start | bytes 1376264 | tf_op jit(solution)/shard_map/ppermute | solution.py:191
  506.2 74.2 %collective-permute-start.58 = (f32[64,1792]{1,0:T(8,128)}, f32[64,1792]{1,0:T(8,128)}, u32[]{:S(2)}, u32[]{:S(2)}) collective-permute-start(f32[64,1792]{1,0:T(8,128)} %get-tuple-element.433), channel_id=1, source_target_pairs={{0,8},{8,16},{16,24},{1,9},{9,17},{17,25},{2,10},{10,18},{18,26},{... | collective-permute-start | bytes 1376264 | tf_op jit(solution)/shard_map/ppermute | solution.py:190
  514.9 73.9 %collective-permute-start.61 = (f32[64,1792]{1,0:T(8,128)}, f32[64,1792]{1,0:T(8,128)}, u32[]{:S(2)}, u32[]{:S(2)}) collective-permute-start(f32[64,1792]{1,0:T(8,128)} %get-tuple-element.430), channel_id=1, source_target_pairs={{8,0},{16,8},{24,16},{9,1},{17,9},{25,17},{10,2},{18,10},{26,18},{... | collective-permute-start | bytes 1376264 | tf_op jit(solution)/shard_map/ppermute | solution.py:191
  522.9 142.8 %collective-permute-start.66 = (f32[2,64,1792]{2,1,0:T(8,128)}, f32[2,64,1792]{2,1,0:T(8,128)}, u32[]{:S(2)}, u32[]{:S(2)}) collective-permute-start(f32[2,64,1792]{2,1,0:T(8,128)} %pad_maximum_fusion.6), channel_id=1, source_target_pairs={{0,3},{1,4},{2,5},{3,6},{4,7},{5,0},{6,1},{7,2},{8,11},{9,12},{10,... | collective-permute-start | bytes 2752520 | tf_op jit(solution)/shard_map/ppermute | solution.py:110
  582.2 74.1 %collective-permute-start.63 = (f32[64,1792]{1,0:T(8,128)S(1)}, f32[64,1792]{1,0:T(8,128)S(1)}, u32[]{:S(2)}, u32[]{:S(2)}) collective-permute-start(f32[64,1792]{1,0:T(8,128)S(1)} %get-tuple-element.428), channel_id=1, source_target_pairs={{8,0},{16,8},{24,16},{9,1},{17,9},{25,17},{10,2},{18,10},{26,18},{... | collective-permute-start | bytes 1376264 | tf_op jit(solution)/shard_map/ppermute | solution.py:191
  700.0 75.1 %collective-permute-start.77 = (f32[64,1792]{1,0:T(8,128)}, f32[64,1792]{1,0:T(8,128)}, u32[]{:S(2)}, u32[]{:S(2)}) collective-permute-start(f32[64,1792]{1,0:T(8,128)} %get-tuple-element.420), channel_id=1, source_target_pairs={{8,0},{16,8},{24,16},{9,1},{17,9},{25,17},{10,2},{18,10},{26,18},{... | collective-permute-start | bytes 1376264 | tf_op jit(solution)/shard_map/ppermute | solution.py:191
  701.3 73.8 %collective-permute-start.76 = (f32[64,1792]{1,0:T(8,128)}, f32[64,1792]{1,0:T(8,128)}, u32[]{:S(2)}, u32[]{:S(2)}) collective-permute-start(f32[64,1792]{1,0:T(8,128)} %get-tuple-element.421), channel_id=1, source_target_pairs={{0,8},{8,16},{16,24},{1,9},{9,17},{17,25},{2,10},{10,18},{18,26},{... | collective-permute-start | bytes 1376264 | tf_op jit(solution)/shard_map/ppermute | solution.py:190
  717.7 142.8 %collective-permute-start.84 = (f32[2,64,1792]{2,1,0:T(8,128)}, f32[2,64,1792]{2,1,0:T(8,128)}, u32[]{:S(2)}, u32[]{:S(2)}) collective-permute-start(f32[2,64,1792]{2,1,0:T(8,128)} %pad_maximum_fusion.8), channel_id=1, source_target_pairs={{0,4},{1,5},{2,6},{3,7},{4,0},{5,1},{6,2},{7,3},{8,12},{9,13},{10,... | collective-permute-start | bytes 2752520 | tf_op jit(solution)/shard_map/ppermute | solution.py:110
  777.0 74.1 %collective-permute-start.81 = (f32[64,1792]{1,0:T(8,128)S(1)}, f32[64,1792]{1,0:T(8,128)S(1)}, u32[]{:S(2)}, u32[]{:S(2)}) collective-permute-start(f32[64,1792]{1,0:T(8,128)S(1)} %get-tuple-element.416), channel_id=1, source_target_pairs={{8,0},{16,8},{24,16},{9,1},{17,9},{25,17},{10,2},{18,10},{26,18},{... | collective-permute-start | bytes 1376264 | tf_op jit(solution)/shard_map/ppermute | solution.py:191
  894.9 74.7 %collective-permute-start.95 = (f32[64,1792]{1,0:T(8,128)}, f32[64,1792]{1,0:T(8,128)}, u32[]{:S(2)}, u32[]{:S(2)}) collective-permute-start(f32[64,1792]{1,0:T(8,128)} %get-tuple-element.408), channel_id=1, source_target_pairs={{8,0},{16,8},{24,16},{9,1},{17,9},{25,17},{10,2},{18,10},{26,18},{... | collective-permute-start | bytes 1376264 | tf_op jit(solution)/shard_map/ppermute | solution.py:191
  912.1 142.8 %collective-permute-start.102 = (f32[2,64,1792]{2,1,0:T(8,128)}, f32[2,64,1792]{2,1,0:T(8,128)}, u32[]{:S(2)}, u32[]{:S(2)}) collective-permute-start(f32[2,64,1792]{2,1,0:T(8,128)} %pad_maximum_fusion.10), channel_id=1, source_target_pairs={{0,5},{1,6},{2,7},{3,0},{4,1},{5,2},{6,3},{7,4},{8,13},{9,14},{10,... | collective-permute-start | bytes 2752520 | tf_op jit(solution)/shard_map/ppermute | solution.py:110
  971.5 74.1 %collective-permute-start.99 = (f32[64,1792]{1,0:T(8,128)S(1)}, f32[64,1792]{1,0:T(8,128)S(1)}, u32[]{:S(2)}, u32[]{:S(2)}) collective-permute-start(f32[64,1792]{1,0:T(8,128)S(1)} %get-tuple-element.404), channel_id=1, source_target_pairs={{8,0},{16,8},{24,16},{9,1},{17,9},{25,17},{10,2},{18,10},{26,18},{... | collective-permute-start | bytes 1376264 | tf_op jit(solution)/shard_map/ppermute | solution.py:191
  1089.4 78.0 %collective-permute-start.113 = (f32[64,1792]{1,0:T(8,128)}, f32[64,1792]{1,0:T(8,128)}, u32[]{:S(2)}, u32[]{:S(2)}) collective-permute-start(f32[64,1792]{1,0:T(8,128)} %get-tuple-element.396), channel_id=1, source_target_pairs={{8,0},{16,8},{24,16},{9,1},{17,9},{25,17},{10,2},{18,10},{26,18},{... | collective-permute-start | bytes 1376264 | tf_op jit(solution)/shard_map/ppermute | solution.py:191
  1090.7 76.7 %collective-permute-start.112 = (f32[64,1792]{1,0:T(8,128)}, f32[64,1792]{1,0:T(8,128)}, u32[]{:S(2)}, u32[]{:S(2)}) collective-permute-start(f32[64,1792]{1,0:T(8,128)} %get-tuple-element.397), channel_id=1, source_target_pairs={{0,8},{8,16},{16,24},{1,9},{9,17},{17,25},{2,10},{10,18},{18,26},{... | collective-permute-start | bytes 1376264 | tf_op jit(solution)/shard_map/ppermute | solution.py:190
  1099.5 76.5 %collective-permute-start.115 = (f32[64,1792]{1,0:T(8,128)}, f32[64,1792]{1,0:T(8,128)}, u32[]{:S(2)}, u32[]{:S(2)}) collective-permute-start(f32[64,1792]{1,0:T(8,128)} %get-tuple-element.394), channel_id=1, source_target_pairs={{8,0},{16,8},{24,16},{9,1},{17,9},{25,17},{10,2},{18,10},{26,18},{... | collective-permute-start | bytes 1376264 | tf_op jit(solution)/shard_map/ppermute | solution.py:191
  1100.8 75.2 %collective-permute-start.114 = (f32[64,1792]{1,0:T(8,128)}, f32[64,1792]{1,0:T(8,128)}, u32[]{:S(2)}, u32[]{:S(2)}) collective-permute-start(f32[64,1792]{1,0:T(8,128)} %get-tuple-element.395), channel_id=1, source_target_pairs={{0,8},{8,16},{16,24},{1,9},{9,17},{17,25},{2,10},{10,18},{18,26},{... | collective-permute-start | bytes 1376264 | tf_op jit(solution)/shard_map/ppermute | solution.py:190
  1107.4 144.7 %collective-permute-start.120 = (f32[2,64,1792]{2,1,0:T(8,128)}, f32[2,64,1792]{2,1,0:T(8,128)}, u32[]{:S(2)}, u32[]{:S(2)}) collective-permute-start(f32[2,64,1792]{2,1,0:T(8,128)} %pad_maximum_fusion.12), channel_id=1, source_target_pairs={{0,6},{1,7},{2,0},{3,1},{4,2},{5,3},{6,4},{7,5},{8,14},{9,15},{10,... | collective-permute-start | bytes 2752520 | tf_op jit(solution)/shard_map/ppermute | solution.py:110
  1322.4 130.9 %collective-permute-start.139 = (f32[64,1792]{1,0:T(8,128)S(1)}, f32[64,1792]{1,0:T(8,128)}, u32[]{:S(2)}, u32[]{:S(2)}) collective-permute-start(f32[64,1792]{1,0:T(8,128)S(1)} %bitcast_subtract_fusion.31.own), channel_id=1, source_target_pairs={{8,0},{16,8},{24,16},{9,1},{17,9},{25,17},{10,2},{18,10},{26,18},{... | collective-permute-start | bytes 1376264 | tf_op jit(solution)/shard_map/ppermute | solution.py:191
  1323.7 129.6 %collective-permute-start.135 = (f32[64,1792]{1,0:T(8,128)S(1)}, f32[64,1792]{1,0:T(8,128)}, u32[]{:S(2)}, u32[]{:S(2)}) collective-permute-start(f32[64,1792]{1,0:T(8,128)S(1)} %bitcast_subtract_fusion.31.own), channel_id=1, source_target_pairs={{0,8},{8,16},{16,24},{1,9},{9,17},{17,25},{2,10},{10,18},{18,26},{... | collective-permute-start | bytes 1376264 | tf_op jit(solution)/shard_map/ppermute | solution.py:190
  1329.7 129.5 %collective-permute-start.141 = (f32[64,1792]{1,0:T(8,128)}, f32[64,1792]{1,0:T(8,128)}, u32[]{:S(2)}, u32[]{:S(2)}) collective-permute-start(f32[64,1792]{1,0:T(8,128)} %collective-permute-done.136.rest_0_), channel_id=1, source_target_pairs={{0,8},{8,16},{16,24},{1,9},{9,17},{17,25},{2,10},{10,18},{18,26},{... | collective-permute-start | bytes 1376264 | tf_op jit(solution)/shard_map/ppermute | solution.py:190
  1335.0 124.2 %collective-permute-start.142 = (f32[64,1792]{1,0:T(8,128)}, f32[64,1792]{1,0:T(8,128)}, u32[]{:S(2)}, u32[]{:S(2)}) collective-permute-start(f32[64,1792]{1,0:T(8,128)} %collective-permute-done.137.rest_3_), channel_id=1, source_target_pairs={{8,0},{16,8},{24,16},{9,1},{17,9},{25,17},{10,2},{18,10},{26,18},{... | collective-permute-start | bytes 1376264 | tf_op jit(solution)/shard_map/ppermute | solution.py:191
  (175 other events, 6259.8 us)

commit v2 on v1

--- a/solution.py
+++ b/solution.py
@@ -21,38 +21,42 @@
 def put_rows(array, matrix, group, lanes, own, from_left, from_right):
     groups = array.shape[1]
     hops = groups - 1
-    q_rows = array.shape[3]
+    parts = [part.reshape((len(lanes),) + array.shape[3:]) for part in (own, *from_left, *from_right)]
 
     def kernel(scalars, own, *rest):
-        left, right, out, sems = rest[:hops], rest[hops : 2 * hops], rest[2 * hops + 1], rest[2 * hops + 2]
+        left, right = rest[:hops], rest[hops : 2 * hops]
+        out, stage, read, written = rest[2 * hops + 1 :]
         group = scalars[0]
 
-        def copies(source, owner, slot):
+        def load(source, slot):
+            return pltpu.make_async_copy(source, stage.at[slot], read.at[slot])
+
+        def stores(slot):
+            owner = group if slot == hops else lax.rem(group + hops - slot, groups)
             return [
-                pltpu.make_async_copy(
-                    source.at[pl.ds(m * q_rows, q_rows)], out.at[matrix, owner, scalars[1 + m]], sems.at[slot, m]
-                )
+                pltpu.make_async_copy(stage.at[slot, m], out.at[matrix, owner, scalars[1 + m]], written.at[slot, m])
                 for m in range(len(lanes))
             ]
 
-        for copy in copies(own, group, hops):
-            copy.start()
+        load(own, hops).start()
         for hop in range(hops):
-            owner = lax.rem(group + hops - hop, groups)
 
             @pl.when(group > hop)
             def _():
-                for copy in copies(left[hop], owner, hop):
-                    copy.start()
+                load(left[hop], hop).start()
 
             @pl.when(group <= hop)
             def _():
-                for copy in copies(right[hops - 1 - hop], owner, hop):
-                    copy.start()
-
-        for slot in range(groups):
-            for copy in copies(own, group, slot):
-                copy.wait()
+                load(right[hops - 1 - hop], hop).start()
+
+        order = [hops, *range(hops)]
+        for slot in order:
+            load(own, slot).wait()
+            for store in stores(slot):
+                store.start()
+        for slot in order:
+            for store in stores(slot):
+                store.wait()
 
     anywhere = pl.BlockSpec(memory_space=pl.ANY)
     size = own.size * 4
@@ -61,10 +65,14 @@
         out_shape=jax.ShapeDtypeStruct(array.shape, array.dtype),
         in_specs=[pl.BlockSpec(memory_space=pltpu.SMEM)] + [anywhere] * (2 * groups),
         out_specs=anywhere,
-        scratch_shapes=[pltpu.SemaphoreType.DMA((groups, len(lanes)))],
+        scratch_shapes=[
+            pltpu.VMEM((groups, len(lanes)) + array.shape[3:], array.dtype),
+            pltpu.SemaphoreType.DMA((groups,)),
+            pltpu.SemaphoreType.DMA((groups, len(lanes))),
+        ],
         input_output_aliases={2 * groups: 0},
         cost_estimate=pl.CostEstimate(flops=0, bytes_accessed=2 * groups * size, transcendentals=0),
-    )(jnp.stack([group, *lanes]).astype(jnp.int32), own, *from_left, *from_right, array)
+    )(jnp.stack([group, *lanes]).astype(jnp.int32), *parts, array)
 
 
 def body(inner_weights, start_weights, momentum):

time: 1610 us -> 742 us (0.46)
  Pallas kernels: 918 us -> 47.5 us
    pallas_call x16, Pallas kernels: 918 us -> 47.5 us  [put_rows(): pl.pallas_call(kernel, out_shape=jax.ShapeDtypeStruct(array.shape, array....]
  transfers between devices with their start and end apart: 146 -> 146, of which waited for: 34 -> 34; matrix products, arithmetic and copies ran while one was open for 12% -> 26% of each run, Pallas kernels for 54% -> 6%
where the time goes in v2:
time: 742 us; the launch traced here: 734 us
  starting transfers between devices  431 us (58%)
  other arithmetic  170 us (23%)
  waiting for transfers between devices  50.5 us (7%)
  Pallas kernels  47.5 us (6%)
  local copies, waits for them, and re-layouts  31.7 us (4%)
    ppermute x64, starting transfers between devices, body(): from_left[matrix] = lax.ppermute(to_right, 'grp', rightward)  326 us
    select_n x46, other arithmetic, body(): jnp.where(groups - 1 - group < phase, to_left + own(matrix, left_owner, s...  102 us
    ppermute x64, starting transfers between devices, body(): from_right[matrix] = lax.ppermute(to_left, 'grp', leftward)  82.3 us
    pallas_call x16, Pallas kernels, put_rows(): pl.pallas_call(kernel, out_shape=jax.ShapeDtypeStruct(array.shape, array....  47.5 us
    sub x16, other arithmetic, body(): kept[matrix] = rows_of(start, matrix, group, step) - update  28.3 us
    ppermute x64, waiting for transfers between devices, body(): from_left[matrix] = lax.ppermute(to_right, 'grp', rightward)  24.7 us
    add x16, other arithmetic, body(): new_momentum = MOMENTUM_COEF * old_momentum + mean_diff  23.9 us
    dynamic_update_slice x7, local copies, waits for them, and re-layouts, land(): lax.dynamic_update_slice(array, part[:, None], (0, lane(plane - shift), 0...  15.1 us
  transfers between devices with their start and end apart: 146, of which 34 were waited for; matrix products, arithmetic and copies ran while one was open for 26% of the time, Pallas kernels for 6%

profile of v2, /device:TPU:0, one launch (start us, length us, event | category | flops | bytes accessed | tf_op | source)
XLA Modules:
  0.0 734.1 jit_solution(13320633481824951258)
XLA Ops:
  82.1 5.7 collective-permute-start.15
  113.1 5.8 collective-permute-start.22
  135.7 5.3 collective-permute-start.26
  145.8 5.3 collective-permute-start.28
  167.6 5.3 collective-permute-start.33
  199.1 5.8 collective-permute-start.40
  209.1 5.6 collective-permute-start.42
  224.7 5.3 collective-permute-start.44
  234.8 5.3 collective-permute-start.46
  257.4 5.3 collective-permute-start.51
  289.4 5.8 collective-permute-start.58
  299.4 5.6 collective-permute-start.60
  312.3 5.3 collective-permute-start.62
  322.4 5.3 collective-permute-start.64
  345.0 5.3 collective-permute-start.69
  376.6 5.8 collective-permute-start.76
  386.6 5.3 collective-permute-start.78
  399.2 5.3 collective-permute-start.80
  409.3 5.3 collective-permute-start.82
  431.9 5.3 collective-permute-start.87
  463.5 5.4 collective-permute-start.94
  473.1 5.3 collective-permute-start.96
  485.7 5.3 collective-permute-start.98
  495.8 5.3 collective-permute-start.100
  518.4 5.3 collective-permute-start.105
  550.1 5.8 collective-permute-start.112
  560.1 5.6 collective-permute-start.114
  575.5 5.3 collective-permute-start.116
  606.8 5.4 collective-permute-start.123
  663.8 5.3 collective-permute-start.136
  674.2 5.8 collective-permute-start.135
  707.9 8.2 %collective-permute-done.143 = f32[64,1792]{1,0:T(8,128)S(1)} collective-permute-done((f32[64,1792]{1,0:T(8,128)}, f32[64,1792]{1,0:T(8,128)S(1)}, u32[]{:S(2)}, u32[]{:S(2)}) %collective-permute-start.143) | collective-permute-done | bytes 458784 | tf_op jit(solution)/shard_map/ppermute | solution.py:199
  (529 shorter events, 553.5 us)
Async XLA Ops:
  71.1 20.5 %collective-permute-start.14 = (f32[64,1792]{1,0:T(8,128)}, f32[64,1792]{1,0:T(8,128)S(1)}, u32[]{:S(2)}, u32[]{:S(2)}) collective-permute-start(f32[64,1792]{1,0:T(8,128)} %bitcast_subtract_fusion.3), channel_id=1, source_target_pairs={{8,0},{16,8},{24,16},{9,1},{17,9},{25,17},{10,2},{18,10},{26,18},{... | collective-permute-start | bytes 1376264 | tf_op jit(solution)/shard_map/ppermute | solution.py:199
  89.1 20.0 %collective-permute-start.19 = (f32[2,64,1792]{2,1,0:T(8,128)S(1)}, f32[2,64,1792]{2,1,0:T(8,128)S(1)}, u32[]{:S(2)}, u32[]{:S(2)}) collective-permute-start(f32[2,64,1792]{2,1,0:T(8,128)S(1)} %pad_maximum_fusion.1), channel_id=1, source_target_pairs={{0,6},{1,7},{2,0},{3,1},{4,2},{5,3},{6,4},{7,5},{8,14},{9,15},{10,... | collective-permute-start | bytes 2752520 | tf_op jit(solution)/shard_map/ppermute | solution.py:118
  111.8 20.7 %collective-permute-start.23 = (f32[64,1792]{1,0:T(8,128)}, f32[64,1792]{1,0:T(8,128)}, u32[]{:S(2)}, u32[]{:S(2)}) collective-permute-start(f32[64,1792]{1,0:T(8,128)} %get-tuple-element.456), channel_id=1, source_target_pairs={{8,0},{16,8},{24,16},{9,1},{17,9},{25,17},{10,2},{18,10},{26,18},{... | collective-permute-start | bytes 1376264 | tf_op jit(solution)/shard_map/ppermute | solution.py:199
  129.4 34.0 %collective-permute-start.30 = (f32[2,64,1792]{2,1,0:T(8,128)}, f32[2,64,1792]{2,1,0:T(8,128)}, u32[]{:S(2)}, u32[]{:S(2)}) collective-permute-start(f32[2,64,1792]{2,1,0:T(8,128)} %pad_maximum_fusion.2), channel_id=1, source_target_pairs={{0,1},{1,2},{2,3},{3,4},{4,5},{5,6},{6,7},{7,0},{8,9},{9,10},{10,1... | collective-permute-start | bytes 2752520 | tf_op jit(solution)/shard_map/ppermute | solution.py:118
  174.2 20.2 %collective-permute-start.37 = (f32[2,64,1792]{2,1,0:T(8,128)S(1)}, f32[2,64,1792]{2,1,0:T(8,128)S(1)}, u32[]{:S(2)}, u32[]{:S(2)}) collective-permute-start(f32[2,64,1792]{2,1,0:T(8,128)S(1)} %pad_maximum_fusion.3), channel_id=1, source_target_pairs={{0,5},{1,6},{2,7},{3,0},{4,1},{5,2},{6,3},{7,4},{8,13},{9,14},{10,... | collective-permute-start | bytes 2752520 | tf_op jit(solution)/shard_map/ppermute | solution.py:118
  197.8 23.7 %collective-permute-start.41 = (f32[64,1792]{1,0:T(8,128)}, f32[64,1792]{1,0:T(8,128)}, u32[]{:S(2)}, u32[]{:S(2)}) collective-permute-start(f32[64,1792]{1,0:T(8,128)} %get-tuple-element.444), channel_id=1, source_target_pairs={{8,0},{16,8},{24,16},{9,1},{17,9},{25,17},{10,2},{18,10},{26,18},{... | collective-permute-start | bytes 1376264 | tf_op jit(solution)/shard_map/ppermute | solution.py:199
  199.1 22.4 %collective-permute-start.40 = (f32[64,1792]{1,0:T(8,128)}, f32[64,1792]{1,0:T(8,128)}, u32[]{:S(2)}, u32[]{:S(2)}) collective-permute-start(f32[64,1792]{1,0:T(8,128)} %get-tuple-element.445), channel_id=1, source_target_pairs={{0,8},{8,16},{16,24},{1,9},{9,17},{17,25},{2,10},{10,18},{18,26},{... | collective-permute-start | bytes 1376264 | tf_op jit(solution)/shard_map/ppermute | solution.py:198
  207.8 22.2 %collective-permute-start.43 = (f32[64,1792]{1,0:T(8,128)}, f32[64,1792]{1,0:T(8,128)}, u32[]{:S(2)}, u32[]{:S(2)}) collective-permute-start(f32[64,1792]{1,0:T(8,128)} %get-tuple-element.442), channel_id=1, source_target_pairs={{8,0},{16,8},{24,16},{9,1},{17,9},{25,17},{10,2},{18,10},{26,18},{... | collective-permute-start | bytes 1376264 | tf_op jit(solution)/shard_map/ppermute | solution.py:199
  209.1 20.9 %collective-permute-start.42 = (f32[64,1792]{1,0:T(8,128)}, f32[64,1792]{1,0:T(8,128)}, u32[]{:S(2)}, u32[]{:S(2)}) collective-permute-start(f32[64,1792]{1,0:T(8,128)} %get-tuple-element.443), channel_id=1, source_target_pairs={{0,8},{8,16},{16,24},{1,9},{9,17},{17,25},{2,10},{10,18},{18,26},{... | collective-permute-start | bytes 1376264 | tf_op jit(solution)/shard_map/ppermute | solution.py:198
  215.8 37.5 %collective-permute-start.48 = (f32[2,64,1792]{2,1,0:T(8,128)}, f32[2,64,1792]{2,1,0:T(8,128)}, u32[]{:S(2)}, u32[]{:S(2)}) collective-permute-start(f32[2,64,1792]{2,1,0:T(8,128)} %pad_maximum_fusion.4), channel_id=1, source_target_pairs={{0,2},{1,3},{2,4},{3,5},{4,6},{5,7},{6,0},{7,1},{8,10},{9,11},{10,... | collective-permute-start | bytes 2752520 | tf_op jit(solution)/shard_map/ppermute | solution.py:118
  247.4 20.2 %collective-permute-start.50 = (f32[64,1792]{1,0:T(8,128)}, f32[64,1792]{1,0:T(8,128)S(1)}, u32[]{:S(2)}, u32[]{:S(2)}) collective-permute-start(f32[64,1792]{1,0:T(8,128)} %bitcast_subtract_fusion.11), channel_id=1, source_target_pairs={{8,0},{16,8},{24,16},{9,1},{17,9},{25,17},{10,2},{18,10},{26,18},{... | collective-permute-start | bytes 1376264 | tf_op jit(solution)/shard_map/ppermute | solution.py:199
  288.1 21.0 %collective-permute-start.59 = (f32[64,1792]{1,0:T(8,128)}, f32[64,1792]{1,0:T(8,128)}, u32[]{:S(2)}, u32[]{:S(2)}) collective-permute-start(f32[64,1792]{1,0:T(8,128)} %get-tuple-element.432), channel_id=1, source_target_pairs={{8,0},{16,8},{24,16},{9,1},{17,9},{25,17},{10,2},{18,10},{26,18},{... | collective-permute-start | bytes 1376264 | tf_op jit(solution)/shard_map/ppermute | solution.py:199
  306.0 34.8 %collective-permute-start.66 = (f32[2,64,1792]{2,1,0:T(8,128)}, f32[2,64,1792]{2,1,0:T(8,128)}, u32[]{:S(2)}, u32[]{:S(2)}) collective-permute-start(f32[2,64,1792]{2,1,0:T(8,128)} %pad_maximum_fusion.6), channel_id=1, source_target_pairs={{0,3},{1,4},{2,5},{3,6},{4,7},{5,0},{6,1},{7,2},{8,11},{9,12},{10,... | collective-permute-start | bytes 2752520 | tf_op jit(solution)/shard_map/ppermute | solution.py:118
  321.1 19.8 %collective-permute-start.65 = (f32[64,1792]{1,0:T(8,128)}, f32[64,1792]{1,0:T(8,128)S(1)}, u32[]{:S(2)}, u32[]{:S(2)}) collective-permute-start(f32[64,1792]{1,0:T(8,128)} %bitcast_subtract_fusion.13), channel_id=1, source_target_pairs={{8,0},{16,8},{24,16},{9,1},{17,9},{25,17},{10,2},{18,10},{26,18},{... | collective-permute-start | bytes 1376264 | tf_op jit(solution)/shard_map/ppermute | solution.py:199
  351.6 21.0 %collective-permute-start.73 = (f32[2,64,1792]{2,1,0:T(8,128)S(1)}, f32[2,64,1792]{2,1,0:T(8,128)S(1)}, u32[]{:S(2)}, u32[]{:S(2)}) collective-permute-start(f32[2,64,1792]{2,1,0:T(8,128)S(1)} %pad_maximum_fusion.7), channel_id=1, source_target_pairs={{0,3},{1,4},{2,5},{3,6},{4,7},{5,0},{6,1},{7,2},{8,11},{9,12},{10,... | collective-permute-start | bytes 2752520 | tf_op jit(solution)/shard_map/ppermute | solution.py:118
  375.3 20.7 %collective-permute-start.77 = (f32[64,1792]{1,0:T(8,128)}, f32[64,1792]{1,0:T(8,128)}, u32[]{:S(2)}, u32[]{:S(2)}) collective-permute-start(f32[64,1792]{1,0:T(8,128)} %get-tuple-element.420), channel_id=1, source_target_pairs={{8,0},{16,8},{24,16},{9,1},{17,9},{25,17},{10,2},{18,10},{26,18},{... | collective-permute-start | bytes 1376264 | tf_op jit(solution)/shard_map/ppermute | solution.py:199
  392.9 34.8 %collective-permute-start.84 = (f32[2,64,1792]{2,1,0:T(8,128)}, f32[2,64,1792]{2,1,0:T(8,128)}, u32[]{:S(2)}, u32[]{:S(2)}) collective-permute-start(f32[2,64,1792]{2,1,0:T(8,128)} %pad_maximum_fusion.8), channel_id=1, source_target_pairs={{0,4},{1,5},{2,6},{3,7},{4,0},{5,1},{6,2},{7,3},{8,12},{9,13},{10,... | collective-permute-start | bytes 2752520 | tf_op jit(solution)/shard_map/ppermute | solution.py:118
  421.9 20.1 %collective-permute-start.86 = (f32[64,1792]{1,0:T(8,128)}, f32[64,1792]{1,0:T(8,128)S(1)}, u32[]{:S(2)}, u32[]{:S(2)}) collective-permute-start(f32[64,1792]{1,0:T(8,128)} %bitcast_subtract_fusion.19), channel_id=1, source_target_pairs={{8,0},{16,8},{24,16},{9,1},{17,9},{25,17},{10,2},{18,10},{26,18},{... | collective-permute-start | bytes 1376264 | tf_op jit(solution)/shard_map/ppermute | solution.py:199
  438.5 21.2 %collective-permute-start.91 = (f32[2,64,1792]{2,1,0:T(8,128)S(1)}, f32[2,64,1792]{2,1,0:T(8,128)S(1)}, u32[]{:S(2)}, u32[]{:S(2)}) collective-permute-start(f32[2,64,1792]{2,1,0:T(8,128)S(1)} %pad_maximum_fusion.9), channel_id=1, source_target_pairs={{0,2},{1,3},{2,4},{3,5},{4,6},{5,7},{6,0},{7,1},{8,10},{9,11},{10,... | collective-permute-start | bytes 2752520 | tf_op jit(solution)/shard_map/ppermute | solution.py:118
  462.2 20.3 %collective-permute-start.95 = (f32[64,1792]{1,0:T(8,128)}, f32[64,1792]{1,0:T(8,128)}, u32[]{:S(2)}, u32[]{:S(2)}) collective-permute-start(f32[64,1792]{1,0:T(8,128)} %get-tuple-element.408), channel_id=1, source_target_pairs={{8,0},{16,8},{24,16},{9,1},{17,9},{25,17},{10,2},{18,10},{26,18},{... | collective-permute-start | bytes 1376264 | tf_op jit(solution)/shard_map/ppermute | solution.py:199
  479.4 34.8 %collective-permute-start.102 = (f32[2,64,1792]{2,1,0:T(8,128)}, f32[2,64,1792]{2,1,0:T(8,128)}, u32[]{:S(2)}, u32[]{:S(2)}) collective-permute-start(f32[2,64,1792]{2,1,0:T(8,128)} %pad_maximum_fusion.10), channel_id=1, source_target_pairs={{0,5},{1,6},{2,7},{3,0},{4,1},{5,2},{6,3},{7,4},{8,13},{9,14},{10,... | collective-permute-start | bytes 2752520 | tf_op jit(solution)/shard_map/ppermute | solution.py:118
  525.0 21.1 %collective-permute-start.109 = (f32[2,64,1792]{2,1,0:T(8,128)S(1)}, f32[2,64,1792]{2,1,0:T(8,128)S(1)}, u32[]{:S(2)}, u32[]{:S(2)}) collective-permute-start(f32[2,64,1792]{2,1,0:T(8,128)S(1)} %pad_maximum_fusion.11), channel_id=1, source_target_pairs={{0,1},{1,2},{2,3},{3,4},{4,5},{5,6},{6,7},{7,0},{8,9},{9,10},{10,1... | collective-permute-start | bytes 2752520 | tf_op jit(solution)/shard_map/ppermute | solution.py:118
  548.8 23.6 %collective-permute-start.113 = (f32[64,1792]{1,0:T(8,128)}, f32[64,1792]{1,0:T(8,128)}, u32[]{:S(2)}, u32[]{:S(2)}) collective-permute-start(f32[64,1792]{1,0:T(8,128)} %get-tuple-element.396), channel_id=1, source_target_pairs={{8,0},{16,8},{24,16},{9,1},{17,9},{25,17},{10,2},{18,10},{26,18},{... | collective-permute-start | bytes 1376264 | tf_op jit(solution)/shard_map/ppermute | solution.py:199
  550.1 22.3 %collective-permute-start.112 = (f32[64,1792]{1,0:T(8,128)}, f32[64,1792]{1,0:T(8,128)}, u32[]{:S(2)}, u32[]{:S(2)}) collective-permute-start(f32[64,1792]{1,0:T(8,128)} %get-tuple-element.397), channel_id=1, source_target_pairs={{0,8},{8,16},{16,24},{1,9},{9,17},{17,25},{2,10},{10,18},{18,26},{... | collective-permute-start | bytes 1376264 | tf_op jit(solution)/shard_map/ppermute | solution.py:198
  558.8 22.1 %collective-permute-start.115 = (f32[64,1792]{1,0:T(8,128)}, f32[64,1792]{1,0:T(8,128)}, u32[]{:S(2)}, u32[]{:S(2)}) collective-permute-start(f32[64,1792]{1,0:T(8,128)} %get-tuple-element.394), channel_id=1, source_target_pairs={{8,0},{16,8},{24,16},{9,1},{17,9},{25,17},{10,2},{18,10},{26,18},{... | collective-permute-start | bytes 1376264 | tf_op jit(solution)/shard_map/ppermute | solution.py:199
  560.1 20.8 %collective-permute-start.114 = (f32[64,1792]{1,0:T(8,128)}, f32[64,1792]{1,0:T(8,128)}, u32[]{:S(2)}, u32[]{:S(2)}) collective-permute-start(f32[64,1792]{1,0:T(8,128)} %get-tuple-element.395), channel_id=1, source_target_pairs={{0,8},{8,16},{16,24},{1,9},{9,17},{17,25},{2,10},{10,18},{18,26},{... | collective-permute-start | bytes 1376264 | tf_op jit(solution)/shard_map/ppermute | solution.py:198
  566.7 35.9 %collective-permute-start.120 = (f32[2,64,1792]{2,1,0:T(8,128)}, f32[2,64,1792]{2,1,0:T(8,128)}, u32[]{:S(2)}, u32[]{:S(2)}) collective-permute-start(f32[2,64,1792]{2,1,0:T(8,128)} %pad_maximum_fusion.12), channel_id=1, source_target_pairs={{0,6},{1,7},{2,0},{3,1},{4,2},{5,3},{6,4},{7,5},{8,14},{9,15},{10,... | collective-permute-start | bytes 2752520 | tf_op jit(solution)/shard_map/ppermute | solution.py:118
  650.2 30.0 %collective-permute-start.138 = (f32[2,64,1792]{2,1,0:T(8,128)S(1)}, f32[2,64,1792]{2,1,0:T(8,128)S(1)}, u32[]{:S(2)}, u32[]{:S(2)}) collective-permute-start(f32[2,64,1792]{2,1,0:T(8,128)S(1)} %pad_maximum_fusion.14), channel_id=1, source_target_pairs={{0,7},{1,0},{2,1},{3,2},{4,3},{5,4},{6,5},{7,6},{8,15},{9,8},{10,9... | collective-permute-start | bytes 2752520 | tf_op jit(solution)/shard_map/ppermute | solution.py:118
  672.9 23.0 %collective-permute-start.139 = (f32[64,1792]{1,0:T(8,128)S(1)}, f32[64,1792]{1,0:T(8,128)}, u32[]{:S(2)}, u32[]{:S(2)}) collective-permute-start(f32[64,1792]{1,0:T(8,128)S(1)} %bitcast_subtract_fusion.31), channel_id=1, source_target_pairs={{8,0},{16,8},{24,16},{9,1},{17,9},{25,17},{10,2},{18,10},{26,18},{... | collective-permute-start | bytes 1376264 | tf_op jit(solution)/shard_map/ppermute | solution.py:199
  674.2 21.7 %collective-permute-start.135 = (f32[64,1792]{1,0:T(8,128)S(1)}, f32[64,1792]{1,0:T(8,128)}, u32[]{:S(2)}, u32[]{:S(2)}) collective-permute-start(f32[64,1792]{1,0:T(8,128)S(1)} %bitcast_subtract_fusion.31), channel_id=1, source_target_pairs={{0,8},{8,16},{16,24},{1,9},{9,17},{17,25},{2,10},{10,18},{18,26},{... | collective-permute-start | bytes 1376264 | tf_op jit(solution)/shard_map/ppermute | solution.py:198
  681.2 20.6 %collective-permute-start.141 = (f32[64,1792]{1,0:T(8,128)}, f32[64,1792]{1,0:T(8,128)}, u32[]{:S(2)}, u32[]{:S(2)}) collective-permute-start(f32[64,1792]{1,0:T(8,128)} %collective-permute-done.136), channel_id=1, source_target_pairs={{0,8},{8,16},{16,24},{1,9},{9,17},{17,25},{2,10},{10,18},{18,26},{... | collective-permute-start | bytes 1376264 | tf_op jit(solution)/shard_map/ppermute | solution.py:198
  702.9 22.3 %collective-permute-start.145 = (f32[64,1792]{1,0:T(8,128)S(1)}, f32[64,1792]{1,0:T(8,128)S(1)}, u32[]{:S(2)}, u32[]{:S(2)}) collective-permute-start(f32[64,1792]{1,0:T(8,128)S(1)} %broadcast_select_fusion.1), channel_id=1, source_target_pairs={{16,24},{8,0},{17,25},{9,1},{18,26},{10,2},{19,27},{11,3},{20,28},... | collective-permute-start | bytes 1376264 | tf_op jit(solution)/shard_map/ppermute | solution.py:203
  (180 other events, 3868.2 us)

commit v3 on v0

--- a/solution.py
+++ b/solution.py
@@ -150,12 +150,10 @@
                     outer = [(0, 1), (groups - 1, groups - 2)]
                     ends = [(groups - 2, groups - 1), (1, 0)]
                     from_left[matrix] = from_right[matrix] = lax.ppermute(alone, "grp", outer if turn == 0 else ends)
-                if tick == 0:
-                    transit.append((tick + groups,) + fetch(order[0]))
-                if in_turn == 2 * groups - 2 and turn + 1 < steps:
-                    transit.append((tick + groups,) + fetch(order[turn + 1]))
-                if in_turn == groups - 2 and 0 < turn < steps:
-                    transit.append((tick + groups,) + deliver(order[turn - 1]))
+                if in_turn == 0 and turn < steps:
+                    transit.append((tick + 3,) + fetch(order[turn]))
+                if in_turn == 3 and 0 < turn < steps:
+                    transit.append((tick + 5,) + deliver(order[turn - 1]))
                 if phase == groups:
                     arrived_left[matrix], arrived_right[matrix] = [], []
                 arrived_left[matrix].append(from_left[matrix])

time: 719 us -> 719 us (level)
  starting transfers between devices: 366 us -> 336 us
  other arithmetic: 172 us -> 191 us
  waiting for transfers between devices: 145 us -> 158 us
    ppermute x64, starting transfers between devices: 260 us -> 233 us  [body(): from_left[matrix] = lax.ppermute(to_right, 'grp', rightward)]
    ppermute x64, waiting for transfers between devices: 96.3 us -> 119 us  [body(): from_right[matrix] = lax.ppermute(to_left, 'grp', leftward)]
    select_n x32, other arithmetic: 50.9 us -> 59 us  [body(): jnp.where(groups - 1 - group < phase, to_left + own(matrix, left_owner, s...]
  transfers between devices with their start and end apart: 146 -> 146, of which waited for: 59 -> 70; matrix products, arithmetic and copies ran while one was open for 27% -> 30% of each run, Pallas kernels for 0% -> 0%
where the time goes in v3:
time: 719 us; the launch traced here: 712 us
  starting transfers between devices  336 us (47%)
  other arithmetic  191 us (27%)
  waiting for transfers between devices  158 us (22%)
  local copies, waits for them, and re-layouts  23.8 us (3%)
    ppermute x64, starting transfers between devices, body(): from_left[matrix] = lax.ppermute(to_right, 'grp', rightward)  233 us
    ppermute x64, waiting for transfers between devices, body(): from_right[matrix] = lax.ppermute(to_left, 'grp', leftward)  119 us
    ppermute x64, starting transfers between devices, body(): from_right[matrix] = lax.ppermute(to_left, 'grp', leftward)  83.1 us
    dynamic_update_slice x64, other arithmetic, write_weights(): lax.dynamic_update_slice(array, part[None, None, None], (matrix, owner, l...  71 us
    select_n x32, other arithmetic, body(): jnp.where(groups - 1 - group < phase, to_left + own(matrix, left_owner, s...  59 us
    add x16, other arithmetic, body(): new_momentum = MOMENTUM_COEF * old_momentum + mean_diff  26.5 us
    select_n x14, other arithmetic, body(): jnp.where(group < phase, to_right + own(matrix, right_owner, step), to_ri...  22.3 us
    ppermute x4, waiting for transfers between devices, body(): lax.ppermute(alone, 'grp', outer if turn == 0 else ends)  20.5 us
  transfers between devices with their start and end apart: 146, of which 70 were waited for; matrix products, arithmetic and copies ran while one was open for 30% of the time, Pallas kernels for 0%

profile of v3, /device:TPU:0, one launch (start us, length us, event | category | flops | bytes accessed | tf_op | source)
XLA Modules:
  0.0 711.8 jit_solution(11033660687567157357)
XLA Ops:
  1.9 5.0 collective-permute-start
  19.3 4.4 collective-permute-start.3
  39.0 4.4 collective-permute-start.7
  48.8 4.4 collective-permute-start.9
  60.2 4.4 collective-permute-start.11
  79.3 4.6 collective-permute-start.15
  90.5 4.6 collective-permute-start.19
  101.3 4.6 collective-permute-start.18
  113.4 4.6 collective-permute-start.23
  131.9 4.6 collective-permute-start.26
  143.5 4.6 collective-permute-start.28
  184.5 4.6 collective-permute-start.36
  195.6 4.6 collective-permute-start.41
  215.7 4.6 collective-permute-start.44
  237.4 4.6 collective-permute-start.49
  268.6 4.6 collective-permute-start.54
  280.9 4.6 collective-permute-start.59
  340.8 4.4 collective-permute-start.73
  351.7 4.6 collective-permute-start.72
  363.3 4.6 collective-permute-start.77
  424.6 4.6 collective-permute-start.91
  435.1 4.6 collective-permute-start.90
  439.7 4.9 collective-permute-done.92
  447.5 4.6 collective-permute-start.95
  476.4 4.6 collective-permute-start.100
  519.0 4.6 collective-permute-start.108
  530.4 4.6 collective-permute-start.113
  602.0 4.6 collective-permute-start.126
  612.8 4.6 collective-permute-start.130
  685.5 5.3 collective-permute-done.144
  693.2 7.5 %collective-permute-done.142 = f32[64,1792]{1,0:T(8,128)S(1)} collective-permute-done((f32[64,1792]{1,0:T(8,128)S(1)}, f32[64,1792]{1,0:T(8,128)S(1)}, u32[]{:S(2)}, u32[]{:S(2)}) %collective-permute-start.142) | collective-permute-done | bytes 458784 | tf_op jit(solution)/shard_map/ppermute | solution.py:152
  703.2 6.2 collective-permute-done.145
  (435 shorter events, 557.6 us)
Async XLA Ops:
  8.1 19.5 %collective-permute-start.2 = (f32[2,64,1792]{2,1,0:T(8,128)S(1)}, f32[2,64,1792]{2,1,0:T(8,128)S(1)}, u32[]{:S(2)}, u32[]{:S(2)}) collective-permute-start(f32[2,64,1792]{2,1,0:T(8,128)S(1)} %pad_maximum_fusion), channel_id=1, source_target_pairs={{0,7},{1,0},{2,1},{3,2},{4,3},{5,4},{6,5},{7,6},{8,15},{9,8},{10,9... | collective-permute-start | bytes 2752520 | tf_op jit(solution)/shard_map/ppermute | solution.py:60
  86.4 24.0 %collective-permute-start.21 = (f32[2,64,1792]{2,1,0:T(8,128)S(1)}, f32[2,64,1792]{2,1,0:T(8,128)S(1)}, u32[]{:S(2)}, u32[]{:S(2)}) collective-permute-start(f32[2,64,1792]{2,1,0:T(8,128)S(1)} %pad_maximum_fusion.1), channel_id=1, source_target_pairs={{0,6},{1,7},{2,0},{3,1},{4,2},{5,3},{6,4},{7,5},{8,14},{9,15},{10,... | collective-permute-start | bytes 2752520 | tf_op jit(solution)/shard_map/ppermute | solution.py:60
  100.0 20.3 %collective-permute-start.17 = (f32[64,1792]{1,0:T(8,128)S(1)}, f32[64,1792]{1,0:T(8,128)S(1)}, u32[]{:S(2)}, u32[]{:S(2)}) collective-permute-start(f32[64,1792]{1,0:T(8,128)S(1)} %get-tuple-element.491), channel_id=1, source_target_pairs={{8,0},{16,8},{24,16},{9,1},{17,9},{25,17},{10,2},{18,10},{26,18},{... | collective-permute-start | bytes 1376264 | tf_op jit(solution)/shard_map/ppermute | solution.py:148
  101.3 19.0 %collective-permute-start.18 = (f32[64,1792]{1,0:T(8,128)S(1)}, f32[64,1792]{1,0:T(8,128)S(1)}, u32[]{:S(2)}, u32[]{:S(2)}) collective-permute-start(f32[64,1792]{1,0:T(8,128)S(1)} %get-tuple-element.490), channel_id=1, source_target_pairs={{0,8},{8,16},{16,24},{1,9},{9,17},{17,25},{2,10},{10,18},{18,26},{... | collective-permute-start | bytes 1376264 | tf_op jit(solution)/shard_map/ppermute | solution.py:147
  127.7 34.3 %collective-permute-start.30 = (f32[2,64,1792]{2,1,0:T(8,128)S(1)}, f32[2,64,1792]{2,1,0:T(8,128)S(1)}, u32[]{:S(2)}, u32[]{:S(2)}) collective-permute-start(f32[2,64,1792]{2,1,0:T(8,128)S(1)} %pad_maximum_fusion.2), channel_id=1, source_target_pairs={{0,1},{1,2},{2,3},{3,4},{4,5},{5,6},{6,7},{7,0},{8,9},{9,10},{10,1... | collective-permute-start | bytes 2752520 | tf_op jit(solution)/shard_map/ppermute | solution.py:60
  169.7 20.1 %collective-permute-start.39 = (f32[2,64,1792]{2,1,0:T(8,128)S(1)}, f32[2,64,1792]{2,1,0:T(8,128)S(1)}, u32[]{:S(2)}, u32[]{:S(2)}) collective-permute-start(f32[2,64,1792]{2,1,0:T(8,128)S(1)} %pad_maximum_fusion.3), channel_id=1, source_target_pairs={{0,5},{1,6},{2,7},{3,0},{4,1},{5,2},{6,3},{7,4},{8,13},{9,14},{10,... | collective-permute-start | bytes 2752520 | tf_op jit(solution)/shard_map/ppermute | solution.py:60
  183.2 19.3 %collective-permute-start.35 = (f32[64,1792]{1,0:T(8,128)S(1)}, f32[64,1792]{1,0:T(8,128)S(1)}, u32[]{:S(2)}, u32[]{:S(2)}) collective-permute-start(f32[64,1792]{1,0:T(8,128)S(1)} %get-tuple-element.479), channel_id=1, source_target_pairs={{8,0},{16,8},{24,16},{9,1},{17,9},{25,17},{10,2},{18,10},{26,18},{... | collective-permute-start | bytes 1376264 | tf_op jit(solution)/shard_map/ppermute | solution.py:148
  194.3 19.8 %collective-permute-start.40 = (f32[64,1792]{1,0:T(8,128)S(1)}, f32[64,1792]{1,0:T(8,128)S(1)}, u32[]{:S(2)}, u32[]{:S(2)}) collective-permute-start(f32[64,1792]{1,0:T(8,128)S(1)} %get-tuple-element.477), channel_id=1, source_target_pairs={{8,0},{16,8},{24,16},{9,1},{17,9},{25,17},{10,2},{18,10},{26,18},{... | collective-permute-start | bytes 1376264 | tf_op jit(solution)/shard_map/ppermute | solution.py:148
  195.6 18.5 %collective-permute-start.41 = (f32[64,1792]{1,0:T(8,128)S(1)}, f32[64,1792]{1,0:T(8,128)S(1)}, u32[]{:S(2)}, u32[]{:S(2)}) collective-permute-start(f32[64,1792]{1,0:T(8,128)S(1)} %get-tuple-element.476), channel_id=1, source_target_pairs={{0,8},{8,16},{16,24},{1,9},{9,17},{17,25},{2,10},{10,18},{18,26},{... | collective-permute-start | bytes 1376264 | tf_op jit(solution)/shard_map/ppermute | solution.py:147
  209.0 34.4 %collective-permute-start.48 = (f32[2,64,1792]{2,1,0:T(8,128)S(1)}, f32[2,64,1792]{2,1,0:T(8,128)S(1)}, u32[]{:S(2)}, u32[]{:S(2)}) collective-permute-start(f32[2,64,1792]{2,1,0:T(8,128)S(1)} %pad_maximum_fusion.4), channel_id=1, source_target_pairs={{0,2},{1,3},{2,4},{3,5},{4,6},{5,7},{6,0},{7,1},{8,10},{9,11},{10,... | collective-permute-start | bytes 2752520 | tf_op jit(solution)/shard_map/ppermute | solution.py:60
  237.4 19.2 %collective-permute-start.49 = (f32[64,1792]{1,0:T(8,128)}, f32[64,1792]{1,0:T(8,128)S(1)}, u32[]{:S(2)}, u32[]{:S(2)}) collective-permute-start(f32[64,1792]{1,0:T(8,128)} %get-tuple-element.397), channel_id=1, source_target_pairs={{0,8},{8,16},{16,24},{1,9},{9,17},{17,25},{2,10},{10,18},{18,26},{... | collective-permute-start | bytes 1376264 | tf_op jit(solution)/shard_map/ppermute | solution.py:147
  253.4 20.4 %collective-permute-start.57 = (f32[2,64,1792]{2,1,0:T(8,128)S(1)}, f32[2,64,1792]{2,1,0:T(8,128)S(1)}, u32[]{:S(2)}, u32[]{:S(2)}) collective-permute-start(f32[2,64,1792]{2,1,0:T(8,128)S(1)} %pad_maximum_fusion.5), channel_id=1, source_target_pairs={{0,4},{1,5},{2,6},{3,7},{4,0},{5,1},{6,2},{7,3},{8,12},{9,13},{10,... | collective-permute-start | bytes 2752520 | tf_op jit(solution)/shard_map/ppermute | solution.py:60
  267.3 20.6 %collective-permute-start.53 = (f32[64,1792]{1,0:T(8,128)S(1)}, f32[64,1792]{1,0:T(8,128)S(1)}, u32[]{:S(2)}, u32[]{:S(2)}) collective-permute-start(f32[64,1792]{1,0:T(8,128)S(1)} %get-tuple-element.467), channel_id=1, source_target_pairs={{8,0},{16,8},{24,16},{9,1},{17,9},{25,17},{10,2},{18,10},{26,18},{... | collective-permute-start | bytes 1376264 | tf_op jit(solution)/shard_map/ppermute | solution.py:148
  268.6 19.3 %collective-permute-start.54 = (f32[64,1792]{1,0:T(8,128)S(1)}, f32[64,1792]{1,0:T(8,128)S(1)}, u32[]{:S(2)}, u32[]{:S(2)}) collective-permute-start(f32[64,1792]{1,0:T(8,128)S(1)} %get-tuple-element.466), channel_id=1, source_target_pairs={{0,8},{8,16},{16,24},{1,9},{9,17},{17,25},{2,10},{10,18},{18,26},{... | collective-permute-start | bytes 1376264 | tf_op jit(solution)/shard_map/ppermute | solution.py:147
  293.8 35.4 %collective-permute-start.66 = (f32[2,64,1792]{2,1,0:T(8,128)S(1)}, f32[2,64,1792]{2,1,0:T(8,128)S(1)}, u32[]{:S(2)}, u32[]{:S(2)}) collective-permute-start(f32[2,64,1792]{2,1,0:T(8,128)S(1)} %pad_maximum_fusion.6), channel_id=1, source_target_pairs={{0,3},{1,4},{2,5},{3,6},{4,7},{5,0},{6,1},{7,2},{8,11},{9,12},{10,... | collective-permute-start | bytes 2752520 | tf_op jit(solution)/shard_map/ppermute | solution.py:60
  336.8 23.6 %collective-permute-start.75 = (f32[2,64,1792]{2,1,0:T(8,128)S(1)}, f32[2,64,1792]{2,1,0:T(8,128)S(1)}, u32[]{:S(2)}, u32[]{:S(2)}) collective-permute-start(f32[2,64,1792]{2,1,0:T(8,128)S(1)} %pad_maximum_fusion.7), channel_id=1, source_target_pairs={{0,3},{1,4},{2,5},{3,6},{4,7},{5,0},{6,1},{7,2},{8,11},{9,12},{10,... | collective-permute-start | bytes 2752520 | tf_op jit(solution)/shard_map/ppermute | solution.py:60
  350.4 19.9 %collective-permute-start.71 = (f32[64,1792]{1,0:T(8,128)S(1)}, f32[64,1792]{1,0:T(8,128)S(1)}, u32[]{:S(2)}, u32[]{:S(2)}) collective-permute-start(f32[64,1792]{1,0:T(8,128)S(1)} %get-tuple-element.455), channel_id=1, source_target_pairs={{8,0},{16,8},{24,16},{9,1},{17,9},{25,17},{10,2},{18,10},{26,18},{... | collective-permute-start | bytes 1376264 | tf_op jit(solution)/shard_map/ppermute | solution.py:148
  351.7 18.6 %collective-permute-start.72 = (f32[64,1792]{1,0:T(8,128)S(1)}, f32[64,1792]{1,0:T(8,128)S(1)}, u32[]{:S(2)}, u32[]{:S(2)}) collective-permute-start(f32[64,1792]{1,0:T(8,128)S(1)} %get-tuple-element.454), channel_id=1, source_target_pairs={{0,8},{8,16},{16,24},{1,9},{9,17},{17,25},{2,10},{10,18},{18,26},{... | collective-permute-start | bytes 1376264 | tf_op jit(solution)/shard_map/ppermute | solution.py:147
  376.3 35.1 %collective-permute-start.84 = (f32[2,64,1792]{2,1,0:T(8,128)S(1)}, f32[2,64,1792]{2,1,0:T(8,128)S(1)}, u32[]{:S(2)}, u32[]{:S(2)}) collective-permute-start(f32[2,64,1792]{2,1,0:T(8,128)S(1)} %pad_maximum_fusion.8), channel_id=1, source_target_pairs={{0,4},{1,5},{2,6},{3,7},{4,0},{5,1},{6,2},{7,3},{8,12},{9,13},{10,... | collective-permute-start | bytes 2752520 | tf_op jit(solution)/shard_map/ppermute | solution.py:60
  403.6 19.4 %collective-permute-start.85 = (f32[64,1792]{1,0:T(8,128)}, f32[64,1792]{1,0:T(8,128)S(1)}, u32[]{:S(2)}, u32[]{:S(2)}) collective-permute-start(f32[64,1792]{1,0:T(8,128)} %get-tuple-element.381), channel_id=1, source_target_pairs={{0,8},{8,16},{16,24},{1,9},{9,17},{17,25},{2,10},{10,18},{18,26},{... | collective-permute-start | bytes 1376264 | tf_op jit(solution)/shard_map/ppermute | solution.py:147
  419.5 25.1 %collective-permute-start.93 = (f32[2,64,1792]{2,1,0:T(8,128)S(1)}, f32[2,64,1792]{2,1,0:T(8,128)S(1)}, u32[]{:S(2)}, u32[]{:S(2)}) collective-permute-start(f32[2,64,1792]{2,1,0:T(8,128)S(1)} %pad_maximum_fusion.9), channel_id=1, source_target_pairs={{0,2},{1,3},{2,4},{3,5},{4,6},{5,7},{6,0},{7,1},{8,10},{9,11},{10,... | collective-permute-start | bytes 2752520 | tf_op jit(solution)/shard_map/ppermute | solution.py:60
  433.8 20.6 %collective-permute-start.89 = (f32[64,1792]{1,0:T(8,128)S(1)}, f32[64,1792]{1,0:T(8,128)S(1)}, u32[]{:S(2)}, u32[]{:S(2)}) collective-permute-start(f32[64,1792]{1,0:T(8,128)S(1)} %get-tuple-element.443), channel_id=1, source_target_pairs={{8,0},{16,8},{24,16},{9,1},{17,9},{25,17},{10,2},{18,10},{26,18},{... | collective-permute-start | bytes 1376264 | tf_op jit(solution)/shard_map/ppermute | solution.py:148
  435.1 19.3 %collective-permute-start.90 = (f32[64,1792]{1,0:T(8,128)S(1)}, f32[64,1792]{1,0:T(8,128)S(1)}, u32[]{:S(2)}, u32[]{:S(2)}) collective-permute-start(f32[64,1792]{1,0:T(8,128)S(1)} %get-tuple-element.442), channel_id=1, source_target_pairs={{0,8},{8,16},{16,24},{1,9},{9,17},{17,25},{2,10},{10,18},{18,26},{... | collective-permute-start | bytes 1376264 | tf_op jit(solution)/shard_map/ppermute | solution.py:147
  460.4 35.5 %collective-permute-start.102 = (f32[2,64,1792]{2,1,0:T(8,128)S(1)}, f32[2,64,1792]{2,1,0:T(8,128)S(1)}, u32[]{:S(2)}, u32[]{:S(2)}) collective-permute-start(f32[2,64,1792]{2,1,0:T(8,128)S(1)} %pad_maximum_fusion.10), channel_id=1, source_target_pairs={{0,5},{1,6},{2,7},{3,0},{4,1},{5,2},{6,3},{7,4},{8,13},{9,14},{10,... | collective-permute-start | bytes 2752520 | tf_op jit(solution)/shard_map/ppermute | solution.py:60
  487.8 18.3 %collective-permute-start.103 = (f32[64,1792]{1,0:T(8,128)}, f32[64,1792]{1,0:T(8,128)S(1)}, u32[]{:S(2)}, u32[]{:S(2)}) collective-permute-start(f32[64,1792]{1,0:T(8,128)} %get-tuple-element.373), channel_id=1, source_target_pairs={{0,8},{8,16},{16,24},{1,9},{9,17},{17,25},{2,10},{10,18},{18,26},{... | collective-permute-start | bytes 1376264 | tf_op jit(solution)/shard_map/ppermute | solution.py:147
  503.9 23.6 %collective-permute-start.111 = (f32[2,64,1792]{2,1,0:T(8,128)S(1)}, f32[2,64,1792]{2,1,0:T(8,128)S(1)}, u32[]{:S(2)}, u32[]{:S(2)}) collective-permute-start(f32[2,64,1792]{2,1,0:T(8,128)S(1)} %pad_maximum_fusion.11), channel_id=1, source_target_pairs={{0,1},{1,2},{2,3},{3,4},{4,5},{5,6},{6,7},{7,0},{8,9},{9,10},{10,1... | collective-permute-start | bytes 2752520 | tf_op jit(solution)/shard_map/ppermute | solution.py:60
  517.7 19.6 %collective-permute-start.107 = (f32[64,1792]{1,0:T(8,128)S(1)}, f32[64,1792]{1,0:T(8,128)S(1)}, u32[]{:S(2)}, u32[]{:S(2)}) collective-permute-start(f32[64,1792]{1,0:T(8,128)S(1)} %get-tuple-element.431), channel_id=1, source_target_pairs={{8,0},{16,8},{24,16},{9,1},{17,9},{25,17},{10,2},{18,10},{26,18},{... | collective-permute-start | bytes 1376264 | tf_op jit(solution)/shard_map/ppermute | solution.py:148
  543.3 35.2 %collective-permute-start.120 = (f32[2,64,1792]{2,1,0:T(8,128)S(1)}, f32[2,64,1792]{2,1,0:T(8,128)S(1)}, u32[]{:S(2)}, u32[]{:S(2)}) collective-permute-start(f32[2,64,1792]{2,1,0:T(8,128)S(1)} %pad_maximum_fusion.12), channel_id=1, source_target_pairs={{0,6},{1,7},{2,0},{3,1},{4,2},{5,3},{6,4},{7,5},{8,14},{9,15},{10,... | collective-permute-start | bytes 2752520 | tf_op jit(solution)/shard_map/ppermute | solution.py:60
  600.7 19.0 %collective-permute-start.125 = (f32[64,1792]{1,0:T(8,128)S(1)}, f32[64,1792]{1,0:T(8,128)S(1)}, u32[]{:S(2)}, u32[]{:S(2)}) collective-permute-start(f32[64,1792]{1,0:T(8,128)S(1)} %get-tuple-element.419), channel_id=1, source_target_pairs={{8,0},{16,8},{24,16},{9,1},{17,9},{25,17},{10,2},{18,10},{26,18},{... | collective-permute-start | bytes 1376264 | tf_op jit(solution)/shard_map/ppermute | solution.py:148
  625.9 35.5 %collective-permute-start.137 = (f32[2,64,1792]{2,1,0:T(8,128)S(1)}, f32[2,64,1792]{2,1,0:T(8,128)S(1)}, u32[]{:S(2)}, u32[]{:S(2)}) collective-permute-start(f32[2,64,1792]{2,1,0:T(8,128)S(1)} %pad_maximum_fusion.14), channel_id=1, source_target_pairs={{0,7},{1,0},{2,1},{3,2},{4,3},{5,4},{6,5},{7,6},{8,15},{9,8},{10,9... | collective-permute-start | bytes 2752520 | tf_op jit(solution)/shard_map/ppermute | solution.py:60
  681.1 19.6 %collective-permute-start.142 = (f32[64,1792]{1,0:T(8,128)S(1)}, f32[64,1792]{1,0:T(8,128)S(1)}, u32[]{:S(2)}, u32[]{:S(2)}) collective-permute-start(f32[64,1792]{1,0:T(8,128)S(1)} %broadcast_select_fusion.1), channel_id=1, source_target_pairs={{16,24},{8,0},{17,25},{9,1},{18,26},{10,2},{19,27},{11,3},{20,28},... | collective-permute-start | bytes 1376264 | tf_op jit(solution)/shard_map/ppermute | solution.py:152
  690.9 18.4 %collective-permute-start.145 = (f32[64,1792]{1,0:T(8,128)S(1)}, f32[64,1792]{1,0:T(8,128)S(1)}, u32[]{:S(2)}, u32[]{:S(2)}) collective-permute-start(f32[64,1792]{1,0:T(8,128)S(1)} %broadcast_select_fusion), channel_id=1, source_target_pairs={{16,24},{8,0},{17,25},{9,1},{18,26},{10,2},{19,27},{11,3},{20,28},... | collective-permute-start | bytes 1376264 | tf_op jit(solution)/shard_map/ppermute | solution.py:152
  (120 other events, 1808.6 us)
